TPU v7x, 32 devices: a whole 2x2x4 slice. The times are simulated.
32 devices in a mesh: tm: 8 (over z, y), state: 4 (over x, core).
Axes of the slice: x: 2, y: 2, z: 4, core: 2. Of those that a mesh axis runs over, the one named last changes fastest.
Arguments:
- dynamics: float32 [512, 512], P('state'), may hold values from -1 to 1
- pattern: int32 [4, 4], replicated, may hold values from 0 to 1
- initial_mean: float32 [4, 512], replicated, may hold values from -6 to 6
- observed: float32 [128, 4], P('tm'), may hold values from -6 to 6
- obs_index: int32 [128], P('tm'), may hold values from 0 to 511
- obs_noise: float32 [128], P('tm'), may hold values from 0.5 to 4
Outputs:
- filtered: float32 [128, 4, 512], P('tm', 'state')
- smoothed: float32 [128, 4, 512], P('tm', 'state')
All inputs are finite; a program needn't handle non-finite values.
Results may differ from a plain program's by a relative error of at most 0.0003.
Values sent between devices are 32-bit elements; how exact they have to be, the bound alone decides.
A program may use at most 256 MiB of HBM per device.

v0:
```python
import jax
import jax.numpy as jnp
from jax import lax
from jax.sharding import PartitionSpec as P


def passed_along(block, axis, distance):
    devices = range(lax.axis_size(axis))
    route = [(i - distance, i) for i in devices if i - distance in devices]
    return lax.ppermute(block, axis, route)


def product(left, right):
    return jnp.dot(left, right, precision=lax.Precision.HIGHEST, preferred_element_type=jnp.float32)


def transposed(left, right):
    return lax.dot_general(
        left,
        right,
        (((1,), (1,)), ((), ())),
        precision=lax.Precision.HIGHEST,
        preferred_element_type=jnp.float32,
    )


def select_tree(usable, first_tree, second_tree):

    def select_leaf(first_leaf, second_leaf):
        return jnp.where(usable, first_leaf, second_leaf)

    return jax.tree.map(select_leaf, first_tree, second_tree)


def per_device(dynamics, pattern, initial_mean, observed, obs_index, obs_noise):
    row_count = dynamics.shape[0]
    state_width = dynamics.shape[1]
    blocks = pattern.shape[0]
    block_span = state_width // blocks
    seq_total = initial_mean.shape[0]
    steps_here = observed.shape[0]
    members = lax.axis_size("state")
    member = lax.axis_index("state")
    segments = lax.axis_size("tm")
    segment = lax.axis_index("tm")
    batch_here = seq_total // members
    present = jnp.maximum(pattern, jnp.eye(blocks, dtype=jnp.int32))
    block_mask = jnp.repeat(jnp.repeat(present, block_span, 0), block_span, 1).astype(jnp.float32)
    transition = lax.all_gather(dynamics, "state", axis=0, tiled=True) * block_mask
    kalman_gains = 1.0 / (1.0 + obs_noise)
    state_index = jnp.arange(state_width, dtype=jnp.int32)
    observed_masks = (state_index[None, :] == obs_index[:, None]).astype(jnp.float32)
    scale_factors = 1.0 - kalman_gains[:, None] * observed_masks
    final_local = jnp.arange(steps_here, dtype=jnp.int32) == steps_here - 1
    retain_flags = 1.0 - jnp.where((segment == segments - 1) & final_local, 1.0, 0.0).astype(
        jnp.float32
    )
    first_row = member * row_count
    owned_rows = (
        jnp.arange(row_count, dtype=jnp.int32)[:, None] + first_row == state_index[None, :]
    ).astype(jnp.float32)
    batch_start = member * batch_here
    local_observations = lax.dynamic_slice_in_dim(observed, batch_start, batch_here, 1)

    def combine_rows(earlier_full, later):
        return (
            product(later[0], earlier_full[0]),
            transposed(earlier_full[1], later[0]) + later[1],
        )

    def doubling(element, direction):
        identity = (owned_rows, jnp.zeros((seq_total, row_count), jnp.float32))
        distances = [1]
        for level_turn in range(9):
            if 2**level_turn < segments:
                distances.append(2**level_turn)
        current = element
        for level_turn, distance in enumerate(distances):
            arrived = passed_along(current, "tm", direction * distance)
            if direction > 0:
                usable = segment >= distance
            else:
                usable = segment + distance < segments
            if level_turn == 0:
                current = select_tree(usable, arrived, identity)
            else:
                gathered = (
                    lax.all_gather(arrived[0], "state", axis=0, tiled=True),
                    lax.all_gather(arrived[1], "state", axis=1, tiled=True),
                )
                current = select_tree(usable, combine_rows(gathered, current), current)
        return current

    def entering(element, start_mean, direction):
        map_rows, map_offsets = doubling(element, direction)
        if start_mean is None:
            entry_rows = map_offsets
        else:
            entry_rows = map_offsets + transposed(start_mean, map_rows)
        return lax.all_to_all(entry_rows, "state", split_axis=0, concat_axis=1, tiled=True)

    def filter_portion(carried, inputs):
        row_block, offsets = carried
        hit_mask, scaling, gain_now, obs_now = inputs
        column_now = product(row_block, hit_mask)
        offsets = offsets + gain_now * obs_now[:, None] * column_now[None, :]
        row_block = product(row_block * scaling[None, :], transition)
        return ((row_block, offsets), None)

    initial_shifts = jnp.zeros((seq_total, row_count), jnp.float32)
    (filter_rows, filter_offsets), unused_value = lax.scan(
        filter_portion,
        (owned_rows, initial_shifts),
        (observed_masks, scale_factors, kalman_gains, observed),
        reverse=True,
    )
    filter_input = entering((filter_rows, filter_offsets), initial_mean, 1)

    def forward_sweep(current_state, inputs):
        scaling, hit_mask, gain_now, obs_now = inputs
        current_state = (
            transposed(current_state, transition) * scaling[None, :]
            + gain_now * obs_now[:, None] * hit_mask[None, :]
        )
        return (current_state, current_state)

    unused_value, filtered = lax.scan(
        forward_sweep,
        filter_input,
        (scale_factors, observed_masks, kalman_gains, local_observations),
    )
    flat_means = filtered.reshape(steps_here * batch_here, state_width)
    backward_mapped = product(transposed(flat_means, transition), transition).reshape(
        steps_here, batch_here, state_width
    )
    residual_terms = (
        filtered - retain_flags[:, None, None] * backward_mapped * scale_factors[:, None, :]
    )

    def smoother_update(current_state, inputs):
        scaling, keep_flag, gap_term = inputs
        current_state = keep_flag * product(current_state, transition) * scaling[None, :] + gap_term
        return (current_state, current_state)

    zero_portion = jnp.zeros((batch_here, state_width), jnp.float32)
    local_shifts, unused_value = lax.scan(
        smoother_update, zero_portion, (scale_factors, retain_flags, residual_terms), reverse=True
    )
    smooth_offsets = lax.all_to_all(local_shifts, "state", split_axis=1, concat_axis=0, tiled=True)

    def smoother_portion(row_block, inputs):
        scaling, keep_flag = inputs
        return (keep_flag * transposed(row_block * scaling[None, :], transition), None)

    smoother_rows, unused_value = lax.scan(
        smoother_portion, owned_rows, (scale_factors, retain_flags)
    )
    smoother_input = entering((smoother_rows, smooth_offsets), None, -1)
    unused_value, smoothed = lax.scan(
        smoother_update, smoother_input, (scale_factors, retain_flags, residual_terms), reverse=True
    )
    return (filtered, smoothed)


def solution(mesh):
    return jax.shard_map(
        per_device,
        mesh=mesh,
        in_specs=(P("state", None), P(), P(), P("tm", None), P("tm"), P("tm")),
        out_specs=(P("tm", "state", None), P("tm", "state", None)),
        check_vma=False,
    )
```

profile of v0, /device:TPU:0, one launch (start us, length us, event | category | flops | bytes accessed | tf_op | source)
XLA Modules:
  0.0 428.5 jit_solution(7946237868741336703)
XLA Ops:
  10.4 18.7 %all-gather.7.cloned.1.call-done = f32[512,512]{1,0:T(8,128)} async-done(((f32[128,512]{1,0:T(8,128)}), f32[512,512]{1,0:T(8,128)}) %all-gather.7.cloned.1.call-update) | async-done | bytes 1048592 | tf_op jit(solution)/shard_map/all_gather | solution.py:49
  31.2 39.2 %while.73 = (s32[]{:T(128)}, f32[128,512]{1,0:T(8,128)S(1)}, f32[4,128]{1,0:T(4,128)S(1)}, f32[16,512]{1,0:T(8,128)S(1)}, f32[512,512]{1,0:T(8,128)S(1)}, /*inde...) while((s32[]{:T(128)}, f32[128,512]{1,0:T(8,128)S(1)}, ...), condition=%wide.region_1.2_spmd.clone, body=%wide.region_0.1_spmd.clone.sunk | while | flops 403506688 | bytes 2372815 | solution.py:111
  73.8 39.7 %while.71 = (s32[]{:T(128)}, f32[128,512]{1,0:T(8,128)S(1)}, f32[16]{0:T(128)S(1)}, f32[16,512]{1,0:T(8,128)S(1)}, f32[512,512]{1,0:T(8,128)S(1)}, /*index=5*/s32[]{:T(128)}) while((s32[]{:T(128)}, f32[128,512]{1,0:T(8,128)S(1)}, f32[16]{0:T(128)S(1)}, f32[16,512]{1,0:T(8,128)S(1)}, f32[512,512]{1,0:T(8,128)S(1)}, /*index=5*/s32[]{:T(128)}) %tuple.176), condition=%wide.region_7.8_spmd, body=%wide.region_6.7_spmd.sunk | while | flops 402784256 | bytes 2103385 | solution.py:155
  114.8 8.7 %collective-permute-done.10 = f32[128,512]{1,0:T(8,128)S(1)} collective-permute-done((f32[128,512]{1,0:T(8,128)S(1)}, f32[128,512]{1,0:T(8,128)S(1)}, u32[]{:S(2)}, u32[]{:S(2)}) %collective-permute-start.10) | collective-permute-done | bytes 262176 | tf_op jit(solution)/shard_map/ppermute | solution.py:10
  128.0 4.8 %collective-permute-done.4 = f32[128,512]{1,0:T(8,128)S(1)} collective-permute-done((f32[128,512]{1,0:T(8,128)S(1)}, f32[128,512]{1,0:T(8,128)S(1)}, u32[]{:S(2)}, u32[]{:S(2)}) %collective-permute-start.4) | collective-permute-done | bytes 262176 | tf_op jit(solution)/shard_map/ppermute | solution.py:10
  133.6 16.9 %all-gather.9.cloned.1.call-done = f32[512,512]{1,0:T(8,128)} async-done(((f32[128,512]{1,0:T(8,128)}), f32[512,512]{1,0:T(8,128)}) %all-gather.9.cloned.1.call-update) | async-done | bytes 1048592 | tf_op jit(solution)/shard_map/all_gather | solution.py:88
  155.9 5.9 %collective-permute-done.6 = f32[128,512]{1,0:T(8,128)S(1)} collective-permute-done((f32[128,512]{1,0:T(8,128)S(1)}, f32[128,512]{1,0:T(8,128)S(1)}, u32[]{:S(2)}, u32[]{:S(2)}) %collective-permute-start.6) | collective-permute-done | bytes 262176 | tf_op jit(solution)/shard_map/ppermute | solution.py:10
  163.9 8.2 %collective-permute-done.12 = f32[128,512]{1,0:T(8,128)S(1)} collective-permute-done((f32[128,512]{1,0:T(8,128)S(1)}, f32[128,512]{1,0:T(8,128)S(1)}, u32[]{:S(2)}, u32[]{:S(2)}) %collective-permute-start.12) | collective-permute-done | bytes 262176 | tf_op jit(solution)/shard_map/ppermute | solution.py:10
  172.9 7.5 %all-gather.11.cloned.1.call-done = f32[512,512]{1,0:T(8,128)} async-done(((f32[128,512]{1,0:T(8,128)}), f32[512,512]{1,0:T(8,128)}) %all-gather.11.cloned.1.call-update) | async-done | bytes 1048592 | tf_op jit(solution)/shard_map/all_gather | solution.py:88
  186.7 6.0 %collective-permute-done.7 = f32[128,512]{1,0:T(8,128)S(1)} collective-permute-done((f32[128,512]{1,0:T(8,128)S(1)}, f32[128,512]{1,0:T(8,128)S(1)}, u32[]{:S(2)}, u32[]{:S(2)}) %collective-permute-start.7) | collective-permute-done | bytes 262176 | tf_op jit(solution)/shard_map/ppermute | solution.py:10
  198.1 8.9 %collective-permute-start.1 = (f32[4,128]{1,0:T(4,128)S(1)}, f32[4,128]{1,0:T(4,128)S(1)}, u32[]{:S(2)}, u32[]{:S(2)}) collective-permute-start(f32[4,128]{1,0:T(4,128)S(1)} %broadcast_select_fusion.1), channel_id=1, source_target_pairs={{0,4},{4,8},{8,12},{12,16},{16,20},{20,24},{24,28},{1,5},{5,9},{9,... | collective-permute-start | bytes 6152 | tf_op jit(solution)/shard_map/ppermute | solution.py:10
  208.3 5.2 %all_gather.37 = f32[4,512]{1,0:T(4,128)S(1)} all-gather(f32[4,128]{1,0:T(4,128)S(1)} %collective-permute-done.1), channel_id=1, replica_groups=mesh['tm'=8,'state'=4] {'state'}, dimensions={1}, use_global_device_ids=true | all-gather | bytes 10240 | tf_op jit(solution)/shard_map/all_gather | solution.py:89
  213.7 6.8 %collective-permute-start.3 = (f32[4,128]{1,0:T(4,128)S(1)}, f32[4,128]{1,0:T(4,128)S(1)}, u32[]{:S(2)}, u32[]{:S(2)}) collective-permute-start(f32[4,128]{1,0:T(4,128)S(1)} %fusion.28), channel_id=1, source_target_pairs={{0,8},{4,12},{8,16},{12,20},{16,24},{20,28},{1,9},{5,13},{9,17},{1... | collective-permute-start | bytes 6152 | tf_op jit(solution)/shard_map/ppermute | solution.py:10
  221.8 5.1 %all_gather.38 = f32[4,512]{1,0:T(4,128)S(1)} all-gather(f32[4,128]{1,0:T(4,128)S(1)} %collective-permute-done.3), channel_id=1, replica_groups=mesh['tm'=8,'state'=4] {'state'}, dimensions={1}, use_global_device_ids=true | all-gather | bytes 10240 | tf_op jit(solution)/shard_map/all_gather | solution.py:89
  227.2 5.4 %collective-permute-start.5 = (f32[4,128]{1,0:T(4,128)S(1)}, f32[4,128]{1,0:T(4,128)S(1)}, u32[]{:S(2)}, u32[]{:S(2)}) collective-permute-start(f32[4,128]{1,0:T(4,128)S(1)} %fusion.27), channel_id=1, source_target_pairs={{0,16},{4,20},{8,24},{12,28},{1,17},{5,21},{9,25},{13,29},{2,18},{... | collective-permute-start | bytes 6152 | tf_op jit(solution)/shard_map/ppermute | solution.py:10
  235.9 5.2 %all_gather.40 = f32[4,512]{1,0:T(4,128)S(1)} all-gather(f32[4,128]{1,0:T(4,128)S(1)} %collective-permute-done.5), channel_id=1, replica_groups=mesh['tm'=8,'state'=4] {'state'}, dimensions={1}, use_global_device_ids=true | all-gather | bytes 10240 | tf_op jit(solution)/shard_map/all_gather | solution.py:89
  251.1 55.4 %while.70 = (s32[]{:T(128)}, f32[1,512]{1,0:T(1,128)S(1)}, f32[16,1,512]{2,1,0:T(1,128)S(1)}, f32[512,512]{1,0:T(8,128)S(1)}, f32[16,512]{1,0:T(8,128)S(1)}, /*i...) while((s32[]{:T(128)}, f32[1,512]{1,0:T(1,128)S(1)}, ...), condition=%wide.region_3.4_spmd, body=%wide.region_2.3_spmd.sunk | while | flops 3147267 | bytes 1063041 | solution.py:127
  308.2 30.3 %while.74 = (s32[]{:T(128)}, f32[1,512]{1,0:T(1,128)S(1)}, f32[16]{0:T(128)S(1)}, f32[512,512]{1,0:T(8,128)S(1)}, f32[16,512]{1,0:T(8,128)S(1)}, /*index=5*/f32[...) while((s32[]{:T(128)}, f32[1,512]{1,0:T(1,128)S(1)}, f32[16]{0:T(128)S(1)}, ...), condition=%wide.region_5.6_spmd.clone, body=%wide.region_4.5_spmd.clone.sunk | while | flops 3147780 | bytes 1065095 | solution.py:146
  338.5 6.1 %all_to_all.48 = f32[1,4,128]{2,0,1:T(1,128)S(1)} all-to-all(f32[1,4,128]{2,0,1:T(1,128)S(1)} %bitcast.162), channel_id=1, replica_groups=mesh['tm'=8,'state'=4] {'state'}, dimensions={1} | all-to-all | bytes 4096 | tf_op jit(solution)/shard_map/all_to_all | solution.py:149
  355.8 5.2 %all_gather.43 = f32[4,512]{1,0:T(4,128)S(1)} all-gather(f32[4,128]{1,0:T(4,128)S(1)} %collective-permute-done.9), channel_id=1, replica_groups=mesh['tm'=8,'state'=4] {'state'}, dimensions={1}, use_global_device_ids=true | all-gather | bytes 10240 | tf_op jit(solution)/shard_map/all_gather | solution.py:89
  367.3 5.2 %all_gather.44 = f32[4,512]{1,0:T(4,128)S(1)} all-gather(f32[4,128]{1,0:T(4,128)S(1)} %collective-permute-done.11), channel_id=1, replica_groups=mesh['tm'=8,'state'=4] {'state'}, dimensions={1}, use_global_device_ids=true | all-gather | bytes 10240 | tf_op jit(solution)/shard_map/all_gather | solution.py:89
  379.2 5.2 %all_gather.46 = f32[4,512]{1,0:T(4,128)S(1)} all-gather(f32[4,128]{1,0:T(4,128)S(1)} %collective-permute-done.13), channel_id=1, replica_groups=mesh['tm'=8,'state'=4] {'state'}, dimensions={1}, use_global_device_ids=true | all-gather | bytes 10240 | tf_op jit(solution)/shard_map/all_gather | solution.py:89
  384.6 6.2 %all_to_all.49 = f32[4,1,128]{2,1,0:T(1,128)S(1)} all-to-all(f32[4,1,128]{2,1,0:T(1,128)S(1)} %bitcast.165), channel_id=1, replica_groups=mesh['tm'=8,'state'=4] {'state'}, dimensions={0} | all-to-all | bytes 4096 | tf_op jit(solution)/shard_map/all_to_all | solution.py:100
  390.7 30.3 %while.72 = (s32[]{:T(128)}, f32[1,512]{1,0:T(1,128)S(1)}, f32[16,1,512]{2,1,0:T(1,128)S(1)}, f32[16]{0:T(128)S(1)}, f32[512,512]{1,0:T(8,128)S(1)}, /*index=5*/...) while((s32[]{:T(128)}, f32[1,512]{1,0:T(1,128)S(1)}, f32[16,1,512]{2,1,0:T(1,128)S(1)}, ...), condition=%wide.region_9.10_spmd, body=%wide.region_8.9_spmd.sunk | while | flops 3147267 | bytes 1067133 | solution.py:159
  (473 shorter events, 269.6 us)
Async XLA Ops:
  7.2 235.8 %copy-start = (f32[4,512]{1,0:T(4,128)S(1)}, f32[4,512]{1,0:T(4,128)}, u32[]{:S(2)}) copy-start(f32[4,512]{1,0:T(4,128)} %param.18) | copy-start | bytes 24580
  7.2 21.9 %all-gather.7.cloned.1.call-start = ((), (), s32[]{:S(2)}) async-start(), calls=%async_computation.3 | async-start | bytes 1310720 | tf_op jit(solution)/shard_map/all_gather | solution.py:49
  7.9 142.6 %all-gather.9.cloned.1.call-start = ((), (), s32[]{:S(2)}) async-start(), calls=%async_computation.4 | async-start | bytes 1310720 | tf_op jit(solution)/shard_map/all_gather | solution.py:88
  31.2 42.6 %copy-start.2 = (f32[128,512]{1,0:T(8,128)S(1)}, f32[128,512]{1,0:T(8,128)}, u32[]{:S(2)}) copy-start(f32[128,512]{1,0:T(8,128)} %copy-done.1) | copy-start | bytes 786436
  70.4 44.4 %collective-permute-start.2 = (f32[128,512]{1,0:T(8,128)S(1)}, f32[128,512]{1,0:T(8,128)S(1)}, u32[]{:S(2)}, u32[]{:S(2)}) collective-permute-start(f32[128,512]{1,0:T(8,128)S(1)} %get-tuple-element.496), channel_id=1, source_target_pairs={{0,4},{4,8},{8,12},{12,16},{16,20},{20,24},{24,28},{1,5},{5,9},{9,... | collective-permute-start | bytes 786440 | tf_op jit(solution)/shard_map/ppermute | solution.py:10
  113.5 10.1 %collective-permute-start.10 = (f32[128,512]{1,0:T(8,128)S(1)}, f32[128,512]{1,0:T(8,128)S(1)}, u32[]{:S(2)}, u32[]{:S(2)}) collective-permute-start(f32[128,512]{1,0:T(8,128)S(1)} %get-tuple-element.499), channel_id=1, source_target_pairs={{4,0},{8,4},{12,8},{16,12},{20,16},{24,20},{28,24},{5,1},{9,5},{13... | collective-permute-start | bytes 786440 | tf_op jit(solution)/shard_map/ppermute | solution.py:10
  123.7 9.1 %collective-permute-start.4 = (f32[128,512]{1,0:T(8,128)S(1)}, f32[128,512]{1,0:T(8,128)S(1)}, u32[]{:S(2)}, u32[]{:S(2)}) collective-permute-start(f32[128,512]{1,0:T(8,128)S(1)} %get-tuple-element.664), channel_id=1, source_target_pairs={{0,4},{4,8},{8,12},{12,16},{16,20},{20,24},{24,28},{1,5},{5,9},{9,... | collective-permute-start | bytes 786440 | tf_op jit(solution)/shard_map/ppermute | solution.py:10
  133.5 46.9 %all-gather.11.cloned.1.call-start = ((), (), s32[]{:S(2)}) async-start(), calls=%async_computation.5 | async-start | bytes 1310720 | tf_op jit(solution)/shard_map/all_gather | solution.py:88
  152.5 9.3 %collective-permute-start.6 = (f32[128,512]{1,0:T(8,128)S(1)}, f32[128,512]{1,0:T(8,128)S(1)}, u32[]{:S(2)}, u32[]{:S(2)}) collective-permute-start(f32[128,512]{1,0:T(8,128)S(1)} %convolution_select_fusion.4), channel_id=1, source_target_pairs={{0,8},{4,12},{8,16},{12,20},{16,24},{20,28},{1,9},{5,13},{9,17},{1... | collective-permute-start | bytes 786440 | tf_op jit(solution)/shard_map/ppermute | solution.py:10
  162.5 70.1 %all-gather.15.cloned.1.call-start = ((), (), s32[]{:S(2)}) async-start(), calls=%async_computation.7 | async-start | bytes 1310720 | tf_op jit(solution)/shard_map/all_gather | solution.py:88
  162.6 9.5 %collective-permute-start.12 = (f32[128,512]{1,0:T(8,128)S(1)}, f32[128,512]{1,0:T(8,128)S(1)}, u32[]{:S(2)}, u32[]{:S(2)}) collective-permute-start(f32[128,512]{1,0:T(8,128)S(1)} %get-tuple-element.663), channel_id=1, source_target_pairs={{4,0},{8,4},{12,8},{16,12},{20,16},{24,20},{28,24},{5,1},{9,5},{13... | collective-permute-start | bytes 786440 | tf_op jit(solution)/shard_map/ppermute | solution.py:10
  172.8 68.2 %all-gather.13.cloned.1.call-start = ((), (), s32[]{:S(2)}) async-start(), calls=%async_computation.6 | async-start | bytes 1310720 | tf_op jit(solution)/shard_map/all_gather | solution.py:88
  182.3 10.3 %collective-permute-start.7 = (f32[128,512]{1,0:T(8,128)S(1)}, f32[128,512]{1,0:T(8,128)S(1)}, u32[]{:S(2)}, u32[]{:S(2)}) collective-permute-start(f32[128,512]{1,0:T(8,128)S(1)} %convolution_select_fusion.3), channel_id=1, source_target_pairs={{0,16},{4,20},{8,24},{12,28},{1,17},{5,21},{9,25},{13,29},{2,18},{... | collective-permute-start | bytes 786440 | tf_op jit(solution)/shard_map/ppermute | solution.py:10
  193.4 4.7 %collective-permute-start = (f32[4,128]{1,0:T(4,128)S(1)}, f32[4,128]{1,0:T(4,128)S(1)}, u32[]{:S(2)}, u32[]{:S(2)}) collective-permute-start(f32[4,128]{1,0:T(4,128)S(1)} %get-tuple-element.495), channel_id=1, source_target_pairs={{0,4},{4,8},{8,12},{12,16},{16,20},{20,24},{24,28},{1,5},{5,9},{9,... | collective-permute-start | bytes 6152 | tf_op jit(solution)/shard_map/ppermute | solution.py:10
  198.1 10.2 %collective-permute-start.1 = (f32[4,128]{1,0:T(4,128)S(1)}, f32[4,128]{1,0:T(4,128)S(1)}, u32[]{:S(2)}, u32[]{:S(2)}) collective-permute-start(f32[4,128]{1,0:T(4,128)S(1)} %broadcast_select_fusion.1), channel_id=1, source_target_pairs={{0,4},{4,8},{8,12},{12,16},{16,20},{20,24},{24,28},{1,5},{5,9},{9,... | collective-permute-start | bytes 6152 | tf_op jit(solution)/shard_map/ppermute | solution.py:10
  213.7 8.1 %collective-permute-start.3 = (f32[4,128]{1,0:T(4,128)S(1)}, f32[4,128]{1,0:T(4,128)S(1)}, u32[]{:S(2)}, u32[]{:S(2)}) collective-permute-start(f32[4,128]{1,0:T(4,128)S(1)} %fusion.28), channel_id=1, source_target_pairs={{0,8},{4,12},{8,16},{12,20},{16,24},{20,28},{1,9},{5,13},{9,17},{1... | collective-permute-start | bytes 6152 | tf_op jit(solution)/shard_map/ppermute | solution.py:10
  227.2 8.6 %collective-permute-start.5 = (f32[4,128]{1,0:T(4,128)S(1)}, f32[4,128]{1,0:T(4,128)S(1)}, u32[]{:S(2)}, u32[]{:S(2)}) collective-permute-start(f32[4,128]{1,0:T(4,128)S(1)} %fusion.27), channel_id=1, source_target_pairs={{0,16},{4,20},{8,24},{12,28},{1,17},{5,21},{9,25},{13,29},{2,18},{... | collective-permute-start | bytes 6152 | tf_op jit(solution)/shard_map/ppermute | solution.py:10
  234.6 13.0 %collective-permute-start.14 = (f32[128,512]{1,0:T(8,128)S(1)}, f32[128,512]{1,0:T(8,128)S(1)}, u32[]{:S(2)}, u32[]{:S(2)}) collective-permute-start(f32[128,512]{1,0:T(8,128)S(1)} %convolution_select_fusion.1), channel_id=1, source_target_pairs={{8,0},{12,4},{16,8},{20,12},{24,16},{28,20},{9,1},{13,5},{17,9},{2... | collective-permute-start | bytes 786440 | tf_op jit(solution)/shard_map/ppermute | solution.py:10
  244.2 6.9 %all-to-all-start = ((f32[4,1,128]{2,1,0:T(1,128)}), f32[4,1,128]{2,1,0:T(1,128)S(1)}, u32[]{:S(2)}, u32[]{:S(2)}) async-start(f32[4,1,128]{2,1,0:T(1,128)} %bitcast.18), calls=%async_computation | async-start | bytes 4096 | tf_op jit(solution)/shard_map/all_to_all | solution.py:100
  247.5 126.6 %all-gather.17.cloned.1.call-start = ((), (), s32[]{:S(2)}) async-start(), calls=%async_computation.8 | async-start | bytes 1310720 | tf_op jit(solution)/shard_map/all_gather | solution.py:88
  344.5 5.5 %collective-permute-start.8 = (f32[4,128]{1,0:T(4,128)S(1)}, f32[4,128]{1,0:T(4,128)S(1)}, u32[]{:S(2)}, u32[]{:S(2)}) collective-permute-start(f32[4,128]{1,0:T(4,128)S(1)} %bitcast.166), channel_id=1, source_target_pairs={{4,0},{8,4},{12,8},{16,12},{20,16},{24,20},{28,24},{5,1},{9,5},{13... | collective-permute-start | bytes 6152 | tf_op jit(solution)/shard_map/ppermute | solution.py:10
  350.0 5.8 %collective-permute-start.9 = (f32[4,128]{1,0:T(4,128)S(1)}, f32[4,128]{1,0:T(4,128)S(1)}, u32[]{:S(2)}, u32[]{:S(2)}) collective-permute-start(f32[4,128]{1,0:T(4,128)S(1)} %broadcast_select_fusion.2), channel_id=1, source_target_pairs={{4,0},{8,4},{12,8},{16,12},{20,16},{24,20},{28,24},{5,1},{9,5},{13... | collective-permute-start | bytes 6152 | tf_op jit(solution)/shard_map/ppermute | solution.py:10
  361.2 6.1 %collective-permute-start.11 = (f32[4,128]{1,0:T(4,128)S(1)}, f32[4,128]{1,0:T(4,128)S(1)}, u32[]{:S(2)}, u32[]{:S(2)}) collective-permute-start(f32[4,128]{1,0:T(4,128)S(1)} %fusion.24), channel_id=1, source_target_pairs={{8,0},{12,4},{16,8},{20,12},{24,16},{28,20},{9,1},{13,5},{17,9},{2... | collective-permute-start | bytes 6152 | tf_op jit(solution)/shard_map/ppermute | solution.py:10
  372.7 6.4 %collective-permute-start.13 = (f32[4,128]{1,0:T(4,128)S(1)}, f32[4,128]{1,0:T(4,128)S(1)}, u32[]{:S(2)}, u32[]{:S(2)}) collective-permute-start(f32[4,128]{1,0:T(4,128)S(1)} %fusion.23), channel_id=1, source_target_pairs={{16,0},{20,4},{24,8},{28,12},{17,1},{21,5},{25,9},{29,13},{18,2},{... | collective-permute-start | bytes 6152 | tf_op jit(solution)/shard_map/ppermute | solution.py:10
  (14 other events, 10.7 us)
Sparse Core Ops, SparseCore 0:
  9.6 19.4 all-gather.6
  133.6 16.8 all-gather.8
  162.6 17.7 all-gather.10
  181.8 16.7 all-gather.14
  200.0 16.8 all-gather.12
  249.6 18.2 all-gather.16
where the time goes:
time: 430 us; the launch traced here: 429 us
  matrix products  104 us (24%)
  waiting for transfers between devices  101 us (23%)
  local copies, waits for them, and re-layouts  56.7 us (13%)
  other arithmetic  53.3 us (12%)
  starting transfers between devices  52.5 us (12%)
  blocking collectives  43.2 us (10%)
  between operations  14.6 us (3%)
    dot_general x40, matrix products, transposed(): lax.dot_general(left, right, (((1,), (1,)), ((), ())), precision=lax.Prec...  58.6 us
    ppermute x15, waiting for transfers between devices, passed_along(): return lax.ppermute(block, axis, route)  54 us
    ppermute x15, starting transfers between devices, passed_along(): return lax.ppermute(block, axis, route)  49.1 us
    dynamic_slice x112, local copies, waits for them, and re-layouts, per_device(): lax.scan(filter_portion, (owned_rows, initial_shifts), (observed_masks, s...  47.7 us
    dot_general x70, matrix products, product(): jnp.dot(left, right, precision=lax.Precision.HIGHEST, preferred_element_t...  45.6 us
    all_gather x6, blocking collectives, doubling(): lax.all_gather(arrived[1], 'state', axis=1, tiled=True)  30.9 us
    all_gather x5, waiting for transfers between devices, doubling(): lax.all_gather(arrived[0], 'state', axis=0, tiled=True)  24.5 us
    mul x32, other arithmetic, smoother_update(): keep_flag * product(current_state, transition) * scaling[None, :] + gap_term  20.9 us
  transfers between devices with their start and end apart: 22, of which 16 were waited for; matrix products, arithmetic and copies ran while one was open for 32% of the time, Pallas kernels for 0%

commit v1 on v0

v1 whole, which is shorter than its diff:
```python
import functools

import jax
import jax.numpy as jnp
from jax import lax
from jax.experimental import pallas as pl
from jax.experimental.pallas import tpu as pltpu
from jax.sharding import PartitionSpec as P

MESH = pl.DeviceIdType.MESH
PIECES = 4
LANES = 128


def gather_kernel(members, segments, dyn_ref, packed_ref, full_ref, obs_ref,
                  x_send, x_recv, c_send, c_recv, f_send, f_recv, o_send, o_recv):
    me = lax.axis_index("state")
    seg = lax.axis_index("tm")
    rows = dyn_ref.shape[0]
    steps = packed_ref.shape[0]
    far = lax.rem(me + members // 2, members)
    near = me + 1 - 2 * lax.rem(me, 2)
    barrier = pltpu.get_barrier_semaphore()
    pl.semaphore_signal(barrier, inc=1, device_id={"state": far}, device_id_type=MESH)
    pl.semaphore_signal(barrier, inc=1, device_id={"state": near}, device_id_type=MESH)
    for d in range(1, segments):
        pl.semaphore_signal(barrier, inc=1, device_id={"tm": lax.rem(seg + d, segments)}, device_id_type=MESH)
    pl.semaphore_wait(barrier, segments + 1)

    piece = rows // PIECES
    own_start = pl.multiple_of(me * rows, rows)
    far_start = pl.multiple_of(far * rows, rows)
    copies = []
    crossing = []
    for i in range(PIECES):
        copy = pltpu.make_async_remote_copy(
            src_ref=dyn_ref.at[pl.ds(i * piece, piece)],
            dst_ref=full_ref.at[pl.ds(own_start + i * piece, piece)],
            send_sem=x_send.at[i], recv_sem=x_recv.at[i],
            device_id={"state": far}, device_id_type=MESH)
        copy.start()
        crossing.append(copy)
    for d in range(1, segments):
        copy = pltpu.make_async_remote_copy(
            src_ref=packed_ref,
            dst_ref=obs_ref.at[pl.ds(pl.multiple_of(seg * steps, steps), steps)],
            send_sem=o_send.at[d], recv_sem=o_recv.at[d],
            device_id={"tm": lax.rem(seg + d, segments)}, device_id_type=MESH)
        copy.start()
        copies.append(copy)
    copy = pltpu.make_async_remote_copy(
        src_ref=dyn_ref, dst_ref=full_ref.at[pl.ds(own_start, rows)],
        send_sem=c_send, recv_sem=c_recv,
        device_id={"state": near}, device_id_type=MESH)
    copy.start()
    copies.append(copy)
    full_ref[pl.ds(own_start, rows)] = dyn_ref[...]
    obs_ref[pl.ds(pl.multiple_of(seg * steps, steps), steps)] = packed_ref[...]
    for i in range(PIECES):
        crossing[i].wait_recv()
        spot = pl.ds(far_start + i * piece, piece)
        copy = pltpu.make_async_remote_copy(
            src_ref=full_ref.at[spot], dst_ref=full_ref.at[spot],
            send_sem=f_send.at[i], recv_sem=f_recv.at[i],
            device_id={"state": near}, device_id_type=MESH)
        copy.start()
        copies.append(copy)
    for copy in crossing:
        copy.wait_send()
    for copy in copies:
        copy.wait()


def halves(value):
    high = value.astype(jnp.bfloat16)
    low = (value - high.astype(jnp.float32)).astype(jnp.bfloat16)
    return high, low


def contract(left, right, dims):
    return lax.dot_general(left, right, (dims, ((), ())), preferred_element_type=jnp.float32)


def multiply(left, right, dims=((1,), (0,))):
    return (contract(left[0], right[1], dims) + contract(left[1], right[0], dims)) + contract(
        left[0], right[0], dims)


TRANS = ((1,), (1,))


def few_rows(left, right, dims=((1,), (0,))):
    count = left.shape[0]
    high = left.astype(jnp.bfloat16).astype(jnp.float32)
    both = jnp.concatenate([high, left - high], axis=0).astype(jnp.bfloat16)
    total = contract(both, right[1], dims) + contract(both, right[0], dims)
    return total[:count] + total[count:]


def compute_kernel(steps, full_ref, pattern_ref, mean_ref, obs_ref, filt_ref, smooth_ref,
                   power_hi, power_lo, powert_hi, powert_lo, r_hi, r_lo, p_hi, p_lo, h_hi, h_lo,
                   scaled_ref, obs_in_ref, hr_hi, hr_lo, u_ref, v_ref, x_ref, own_x, own_p):
    width = full_ref.shape[1]
    total = obs_ref.shape[0]
    blocks = pattern_ref.shape[0]
    span = width // blocks
    group = LANES
    groups = total // group
    chunks = total // steps
    per_group = group // steps
    levels = steps.bit_length() - 1
    sequences = mean_ref.shape[0]
    member = lax.axis_index("state")
    segment = lax.axis_index("tm")

    for i in range(blocks):
        for j in range(blocks):
            tile = full_ref[i * span:(i + 1) * span, j * span:(j + 1) * span]
            if i != j:
                tile = tile * jnp.maximum(pattern_ref[i, j], 0).astype(jnp.float32)
            hi, lo = halves(tile)
            power_hi[0, i * span:(i + 1) * span, j * span:(j + 1) * span] = hi
            power_lo[0, i * span:(i + 1) * span, j * span:(j + 1) * span] = lo

    for k in range(levels):
        square = multiply((power_hi[k], power_lo[k]), (power_hi[k], power_lo[k]))
        power_hi[k + 1], power_lo[k + 1] = halves(square)
    for k in range(levels + 1):
        powert_hi[k] = power_hi[k].T
        powert_lo[k] = power_lo[k].T

    row = lax.broadcasted_iota(jnp.int32, (group, group), 0)
    col = lax.broadcasted_iota(jnp.int32, (group, group), 1)
    wide = lax.broadcasted_iota(jnp.int32, (group, width), 1)
    row_wide = lax.broadcasted_iota(jnp.int32, (group, width), 0)

    def prepare(g):
        here = pl.ds(pl.multiple_of(g * group, group), group)
        packed = obs_ref[here, :]
        index = jnp.sum(jnp.where(col == sequences, packed, 0.0), axis=1, keepdims=True).astype(jnp.int32)
        noise = jnp.sum(jnp.where(col == sequences + 1, packed, 0.0), axis=1, keepdims=True)
        observed = jnp.sum(jnp.where(col == member, packed, 0.0), axis=1, keepdims=True)
        root = jnp.sqrt(1.0 / (1.0 + noise))
        scaled = jnp.where(wide == index, root, 0.0)
        scaled_ref[here, :] = scaled
        p_now = scaled
        r_now = multiply(halves(scaled), (power_hi[0], power_lo[0]))
        inverse = jnp.where(row == col, 1.0, 0.0)
        for k in range(levels):
            r_pair = halves(r_now)
            p_pair = halves(p_now)
            r_hi[k, here, :], r_lo[k, here, :] = r_pair
            p_hi[k, here, :], p_lo[k, here, :] = p_pair
            gram = multiply(r_pair, p_pair, TRANS)
            size = 2**k
            sibling = ((row // (2 * size)) == (col // (2 * size))) & ((row // size) == (col // size) + 1)
            gram = jnp.where(sibling, gram, 0.0)
            if k == 0:
                inverse = inverse - gram
            else:
                pair = halves(inverse)
                inverse = inverse - multiply(halves(multiply(pair, halves(gram))), pair)
            set_bit = ((row_wide // size) % 2) == 1
            r_now = jnp.where(set_bit, multiply(r_pair, (power_hi[k], power_lo[k])), r_now)
            p_now = jnp.where(set_bit, p_now, multiply(p_pair, (powert_hi[k], powert_lo[k])))
        r_pair = halves(r_now)
        r_hi[levels, here, :], r_lo[levels, here, :] = r_pair
        p_hi[levels, here, :], p_lo[levels, here, :] = halves(p_now)
        pair = halves(inverse)
        h_hi[here, :], h_lo[here, :] = pair
        hr_hi[here, :], hr_lo[here, :] = halves(multiply(pair, r_pair))
        source = multiply(pair, halves(jnp.where(col == member, observed * root, 0.0)))
        obs_in_ref[here, :] = jnp.broadcast_to(
            jnp.sum(source.T, axis=0, keepdims=True), (group, group))

    if groups == 1:
        prepare(0)
    else:
        lax.fori_loop(0, groups, lambda g, c: (prepare(g), c)[1], 0)

    lane8 = lax.broadcasted_iota(jnp.int32, (8, group), 1)
    u_ref[...] = jnp.zeros_like(u_ref)
    v_ref[...] = jnp.zeros_like(v_ref)
    top = (power_hi[levels], power_lo[levels])
    top_t = (powert_hi[levels], powert_lo[levels])

    def here_of(c):
        g = c // per_group
        return pl.ds(pl.multiple_of(g * group, group), group), pl.ds(pl.multiple_of(g * 8, 8), 8), c % per_group

    def forward(c, state):
        here, small, spot = here_of(c)
        x_ref[pl.ds(pl.multiple_of(c * 8, 8), 8), :] = state
        first = pl.ds(pl.multiple_of((c // per_group) * group, group), 8)
        drive = obs_in_ref[first, :] - few_rows(state, (hr_hi[here, :], hr_lo[here, :]), TRANS)
        drive = jnp.where(lane8 // steps == spot, drive, 0.0)
        u_ref[small, :] = u_ref[small, :] + drive
        return few_rows(state, top_t) + few_rows(drive, (p_hi[levels, here, :], p_lo[levels, here, :]))

    mean = jnp.sum(
        jnp.where(lax.broadcasted_iota(jnp.int32, mean_ref.shape, 0) == member, mean_ref[...], 0.0),
        axis=0, keepdims=True)
    state = jnp.broadcast_to(mean, (8, width))
    if chunks <= 8:
        for c in range(chunks):
            state = forward(c, state)
    else:
        state = lax.fori_loop(0, chunks, forward, state)
    x_ref[chunks * 8:(chunks + 1) * 8, :] = state

    def backward(i, state):
        c = chunks - 1 - i
        here, small, spot = here_of(c)
        own_p[pl.ds(pl.multiple_of(c * 8, 8), 8), :] = state
        seen = u_ref[small, :] - few_rows(state, (p_hi[levels, here, :], p_lo[levels, here, :]), TRANS)
        seen = jnp.where(lane8 // steps == spot, seen, 0.0)
        drive = few_rows(seen, (h_hi[here, :], h_lo[here, :]))
        drive = jnp.where(lane8 // steps == spot, drive, 0.0)
        v_ref[small, :] = v_ref[small, :] + drive
        return few_rows(state, top) + few_rows(drive, (r_hi[levels, here, :], r_lo[levels, here, :]))

    state = jnp.zeros((8, width), jnp.float32)
    if chunks <= 8:
        for i in range(chunks):
            state = backward(i, state)
    else:
        state = lax.fori_loop(0, chunks, backward, state)

    here, small, spot = here_of(segment)
    lane = lax.broadcasted_iota(jnp.int32, (steps, group), 1)
    tau = lax.broadcasted_iota(jnp.int32, (steps, group), 0)
    tall = lax.broadcasted_iota(jnp.int32, (steps, width), 0)
    local = lane - spot * steps
    mine = (local >= 0) & (local < steps)
    u_own = jnp.where(mine, jnp.broadcast_to(u_ref[small, :][:1], (steps, group)), 0.0)
    v_own = jnp.where(mine, jnp.broadcast_to(v_ref[small, :][:1], (steps, group)), 0.0)
    enter = x_ref[pl.ds(pl.multiple_of(segment * 8, 8), 8), :][:1]
    leave = x_ref[pl.ds(pl.multiple_of((segment + 1) * 8, 8), 8), :][:1]
    after = own_p[pl.ds(pl.multiple_of(segment * 8, 8), 8), :][:1]
    xs = jnp.where(tall == 0, jnp.broadcast_to(enter, (steps, width)), 0.0)
    ps = jnp.where(tall == steps - 1, jnp.broadcast_to(after, (steps, width)), 0.0)
    for k in reversed(range(levels)):
        size = 2**k
        u_use = jnp.where((local >= tau - size) & (local < tau), u_own, 0.0)
        v_use = jnp.where((local > tau) & (local <= tau + size), v_own, 0.0)
        p_level = (p_hi[k, here, :], p_lo[k, here, :])
        r_level = (r_hi[k, here, :], r_lo[k, here, :])
        moved = few_rows(pltpu.roll(xs, size, 0), (powert_hi[k], powert_lo[k])) + few_rows(u_use, p_level)
        xs = jnp.where(tall % (2 * size) == size, moved, xs)
        moved = few_rows(pltpu.roll(ps, steps - size, 0), (power_hi[k], power_lo[k])) + few_rows(v_use, r_level)
        ps = jnp.where((tall + 1) % (2 * size) == size, moved, ps)
    xs = jnp.where(tall == steps - 1, jnp.broadcast_to(leave, (steps, width)), pltpu.roll(xs, steps - 1, 0))
    hits = scaled_ref[pl.ds(pl.multiple_of(segment * steps, steps), steps), :]
    change = jnp.sum(jnp.where(local == tau, v_own - u_own, 0.0), axis=1, keepdims=True)
    filt_ref[...] = xs
    smooth_ref[...] = xs + ps + hits * change


def per_device(dynamics, pattern, initial_mean, observed, obs_index, obs_noise):
    rows, width = dynamics.shape
    sequences = initial_mean.shape[0]
    steps = observed.shape[0]
    members = lax.axis_size("state")
    segments = lax.axis_size("tm")
    total = steps * segments
    levels = steps.bit_length() - 1
    groups = total // LANES
    chunks = segments
    packed = jnp.concatenate(
        [observed, obs_index.astype(jnp.float32)[:, None], obs_noise[:, None],
         jnp.zeros((steps, LANES - sequences - 2), jnp.float32)], axis=1)
    vmem = pl.BlockSpec(memory_space=pltpu.VMEM)
    dma = pltpu.SemaphoreType.DMA
    full, gathered = pl.pallas_call(
        functools.partial(gather_kernel, members, segments),
        out_shape=(jax.ShapeDtypeStruct((rows * members, width), jnp.float32),
                   jax.ShapeDtypeStruct((total, LANES), jnp.float32)),
        in_specs=[vmem, vmem],
        out_specs=(vmem, vmem),
        scratch_shapes=[dma((PIECES,)), dma((PIECES,)), dma, dma, dma((PIECES,)), dma((PIECES,)),
                        dma((segments,)), dma((segments,))],
        compiler_params=pltpu.CompilerParams(collective_id=0, has_side_effects=True),
        name="gather",
    )(dynamics, packed)
    bf, f32 = jnp.bfloat16, jnp.float32
    out = jax.ShapeDtypeStruct((steps, width), f32)
    filtered, smoothed = pl.pallas_call(
        functools.partial(compute_kernel, steps),
        out_shape=(out, out),
        in_specs=[vmem, pl.BlockSpec(memory_space=pltpu.SMEM), vmem, vmem],
        out_specs=(vmem, vmem),
        scratch_shapes=(
            [pltpu.VMEM((levels + 1, width, width), bf)] * 4
            + [pltpu.VMEM((levels + 1, total, width), bf)] * 4
            + [pltpu.VMEM((total, LANES), bf)] * 2
            + [pltpu.VMEM((total, width), f32), pltpu.VMEM((total, LANES), f32)]
            + [pltpu.VMEM((total, width), bf)] * 2
            + [pltpu.VMEM((8 * groups, LANES), f32)] * 2
            + [pltpu.VMEM((8 * (chunks + 1), width), f32)] * 3),
        compiler_params=pltpu.CompilerParams(vmem_limit_bytes=56 * 1024 * 1024),
        name="smooth",
    )(full, pattern, initial_mean, gathered)
    return filtered[:, None, :], smoothed[:, None, :]


def solution(mesh):
    return jax.shard_map(
        per_device,
        mesh=mesh,
        in_specs=(P("state", None), P(), P(), P("tm", None), P("tm"), P("tm")),
        out_specs=(P("tm", "state", None), P("tm", "state", None)),
        check_vma=False,
    )
```

time: 430 us -> 40.8 us (0.09)
  matrix products: 104 us -> 0 us
  waiting for transfers between devices: 101 us -> 0 us
  other arithmetic: 53.3 us -> 0.68 us
  starting transfers between devices: 52.5 us -> 0 us
  local copies, waits for them, and re-layouts: 56.7 us -> 4.21 us
  blocking collectives: 43.2 us -> 0 us
  Pallas kernels: 0 us -> 35 us
  between operations: 14.6 us -> 0.65 us
    dot_general x110 -> x0, matrix products: 104 us -> none  [the longest x40 58.6 us: transposed(): lax.dot_general(left, right, (((1,), (1,)), ((), ())), precision=lax.Prec...]
    ppermute x15 -> x0, waiting for transfers between devices: 54 us -> none  [passed_along(): return lax.ppermute(block, axis, route)]
    mul x65 -> x0, other arithmetic: 51.1 us -> none  [the longest x32 20.9 us: smoother_update(): keep_flag * product(current_state, transition) * scaling[None, :] + gap_term]
    ppermute x15 -> x0, starting transfers between devices: 49.1 us -> none  [passed_along(): return lax.ppermute(block, axis, route)]
    dynamic_slice x113 -> x0, local copies, waits for them, and re-layouts: 47.7 us -> none  [the longest x112 47.7 us: per_device(): lax.scan(filter_portion, (owned_rows, initial_shifts), (observed_masks, s...]
    all_gather x6 -> x0, waiting for transfers between devices: 43.2 us -> none  [the longest x5 24.5 us: doubling(): lax.all_gather(arrived[0], 'state', axis=0, tiled=True)]
    pallas_call x0 -> x2, Pallas kernels: none -> 35 us  [the longest x1 18.3 us: per_device(): pl.pallas_call(functools.partial(compute_kernel, steps), out_shape=(out,...]
    all_gather x6 -> x0, blocking collectives: 30.9 us -> none  [doubling(): lax.all_gather(arrived[1], 'state', axis=1, tiled=True)]
  transfers between devices with their start and end apart: 22 -> 0, of which waited for: 16 -> 0; matrix products, arithmetic and copies ran while one was open for 32% -> 0% of each run, Pallas kernels for 0% -> 0%
where the time goes in v1:
time: 40.8 us; the launch traced here: 40.5 us
  Pallas kernels  35 us (86%)
  local copies, waits for them, and re-layouts  4.21 us (10%)
  other arithmetic  0.68 us (2%)
  between operations  0.65 us (2%)
    pallas_call x1, Pallas kernels, per_device(): pl.pallas_call(functools.partial(compute_kernel, steps), out_shape=(out,...  18.3 us
    pallas_call x1, Pallas kernels, per_device(): pl.pallas_call(functools.partial(gather_kernel, members, segments), out_s...  16.7 us
    unnamed x11, local copies, waits for them, and re-layouts  3.97 us

profile of v1, /device:TPU:0, one launch (start us, length us, event | category | flops | bytes accessed | tf_op | source)
XLA Modules:
  0.0 40.5 jit_solution(7576046694161792595)
XLA Ops:
  0.6 0.0 copy-start.3
  0.6 0.6 %copy-done.3 = s32[16]{0:T(128)S(1)} copy-done((s32[16]{0:T(128)S(1)}, s32[16]{0:T(128)}, u32[]{:S(2)}) %copy-start.3) | copy-done | bytes 88
  1.3 0.1 pad.3.clone
  1.4 0.0 copy-start.1
  1.4 0.1 copy.9
  1.5 0.6 %copy-done.1 = f32[16,4]{0,1:T(4,128)S(1)} copy-done((f32[16,4]{0,1:T(4,128)S(1)}, f32[16,4]{0,1:T(4,128)}, u32[]{:S(2)}) %copy-start.1) | copy-done | bytes 280
  2.1 0.0 copy-start.2
  2.1 0.1 copy.8
  2.1 0.6 %copy-done.2 = f32[16]{0:T(128)S(1)} copy-done((f32[16]{0:T(128)S(1)}, f32[16]{0:T(128)}, u32[]{:S(2)}) %copy-start.2) | copy-done | bytes 88
  2.7 0.1 copy.10
  2.8 0.7 %maximum_maximum_fusion.packed_ref = f32[16,128]{1,0:T(8,128)} fusion(f32[16,1]{1,0:T(8,128)S(1)} %copy.10, f32[16,1]{1,0:T(8,128)S(1)} %copy.9, f32[16,4]{1,0:T(8,128)S(1)} %copy.8, f32[128]{0:T(128)S(1)} %pad.3.clone), kind=kLoop, calls=%fused_computation | loop fusion | flops 6144 | bytes 9088 | tf_op jit(solution)/shard_map/concatenate | solution.py:269
  3.5 16.7 %gather.1 = (f32[512,512]{1,0:T(8,128)}, f32[128,128]{1,0:T(8,128)}) custom-call(f32[128,512]{1,0:T(8,128)} %dyn_ref.1, f32[16,128]{1,0:T(8,128)} %maximum_maximum_fusion.packed_ref), custom_call_target="tpu_custom_call" | custom-call | tf_op jit(solution)/shard_map/gather/pallas_call | solution.py:274
  20.1 18.3 %smooth.1 = (f32[16,512]{1,0:T(8,128)}, f32[16,512]{1,0:T(8,128)}) custom-call(f32[512,512]{1,0:T(8,128)} %get-tuple-element.6.full_ref, s32[4,4]{1,0:T(4,128)} %pattern_ref.1, f32[4,512]{1,0:T(4,128)} %mean_ref.1, f32[128,128]{1,0:T(8,128)} %get-tuple-element.7.obs_ref), custom_call_target="tpu_custom_call" | custom-call | tf_op jit(solution)/shard_map/smooth/pallas_call | solution.py:287
  38.5 0.0 copy-start
  38.5 1.4 %copy.11 = f32[16,1,512]{2,1,0:T(1,128)} copy(f32[16,1,512]{2,0,1:T(8,128)} %bitcast.6) | data formatting | bytes 65536
  39.9 0.0 copy-done
  39.9 0.6 %copy.12 = f32[16,1,512]{2,1,0:T(1,128)} copy(f32[16,1,512]{2,0,1:T(8,128)S(1)} %bitcast.5) | data formatting | bytes 65536
  (2 shorter events, 0.0 us)
Async XLA Ops:
  0.6 0.7 %copy-start.3 = (s32[16]{0:T(128)S(1)}, s32[16]{0:T(128)}, u32[]{:S(2)}) copy-start(s32[16]{0:T(128)} %param.10) | copy-start | bytes 196
  1.4 0.7 %copy-start.1 = (f32[16,4]{0,1:T(4,128)S(1)}, f32[16,4]{0,1:T(4,128)}, u32[]{:S(2)}) copy-start(f32[16,4]{0,1:T(4,128)} %param.9) | copy-start | bytes 772
  2.1 0.7 %copy-start.2 = (f32[16]{0:T(128)S(1)}, f32[16]{0:T(128)}, u32[]{:S(2)}) copy-start(f32[16]{0:T(128)} %param.11) | copy-start | bytes 196
  38.5 1.4 %copy-start = (f32[16,512]{1,0:T(8,128)S(1)}, f32[16,512]{1,0:T(8,128)}, u32[]{:S(2)}) copy-start(f32[16,512]{1,0:T(8,128)} %get-tuple-element.9) | copy-start | bytes 98308

commit v2 on v1

--- a/solution.py
+++ b/solution.py
@@ -12,60 +12,68 @@
 LANES = 128
 
 
-def gather_kernel(members, segments, dyn_ref, packed_ref, full_ref, obs_ref,
-                  x_send, x_recv, c_send, c_recv, f_send, f_recv, o_send, o_recv):
+def gather_kernel(members, segments, dyn_ref, observed_ref, index_ref, noise_ref, full_ref, obs_ref,
+                  raw_ref, packed_ref, x_send, x_recv, y_send, y_recv, c_send, c_recv,
+                  f_send, f_recv, o_send, o_recv):
     me = lax.axis_index("state")
     seg = lax.axis_index("tm")
     rows = dyn_ref.shape[0]
-    steps = packed_ref.shape[0]
+    sequences, steps = observed_ref.shape
     far = lax.rem(me + members // 2, members)
     near = me + 1 - 2 * lax.rem(me, 2)
+    side = lax.rem(seg, 2)
+    across = seg + 1 - 2 * side
     barrier = pltpu.get_barrier_semaphore()
     pl.semaphore_signal(barrier, inc=1, device_id={"state": far}, device_id_type=MESH)
     pl.semaphore_signal(barrier, inc=1, device_id={"state": near}, device_id_type=MESH)
     for d in range(1, segments):
         pl.semaphore_signal(barrier, inc=1, device_id={"tm": lax.rem(seg + d, segments)}, device_id_type=MESH)
+    raw_ref[...] = jnp.zeros_like(raw_ref)
+    raw_ref[:sequences, :steps] = observed_ref[...]
+    raw_ref[sequences:sequences + 1, :steps] = index_ref[...].astype(jnp.float32)
+    raw_ref[sequences + 1:sequences + 2, :steps] = noise_ref[...]
+    packed_ref[...] = raw_ref[...].T[:steps]
     pl.semaphore_wait(barrier, segments + 1)
 
-    piece = rows // PIECES
+    half = rows // 2
+    piece = half // PIECES
     own_start = pl.multiple_of(me * rows, rows)
     far_start = pl.multiple_of(far * rows, rows)
+    mine = side * half
+    theirs = half - mine
     copies = []
     crossing = []
+    swapping = []
+
+    def send(src, dst, sends, recvs, target):
+        copy = pltpu.make_async_remote_copy(
+            src_ref=src, dst_ref=dst, send_sem=sends, recv_sem=recvs,
+            device_id=target, device_id_type=MESH)
+        copy.start()
+        return copy
+
     for i in range(PIECES):
-        copy = pltpu.make_async_remote_copy(
-            src_ref=dyn_ref.at[pl.ds(i * piece, piece)],
-            dst_ref=full_ref.at[pl.ds(own_start + i * piece, piece)],
-            send_sem=x_send.at[i], recv_sem=x_recv.at[i],
-            device_id={"state": far}, device_id_type=MESH)
-        copy.start()
-        crossing.append(copy)
+        at = pl.multiple_of(mine + i * piece, piece)
+        crossing.append(send(dyn_ref.at[pl.ds(at, piece)],
+                             full_ref.at[pl.ds(pl.multiple_of(own_start + at, piece), piece)],
+                             x_send.at[i], x_recv.at[i], {"state": far}))
     for d in range(1, segments):
-        copy = pltpu.make_async_remote_copy(
-            src_ref=packed_ref,
-            dst_ref=obs_ref.at[pl.ds(pl.multiple_of(seg * steps, steps), steps)],
-            send_sem=o_send.at[d], recv_sem=o_recv.at[d],
-            device_id={"tm": lax.rem(seg + d, segments)}, device_id_type=MESH)
-        copy.start()
-        copies.append(copy)
-    copy = pltpu.make_async_remote_copy(
-        src_ref=dyn_ref, dst_ref=full_ref.at[pl.ds(own_start, rows)],
-        send_sem=c_send, recv_sem=c_recv,
-        device_id={"state": near}, device_id_type=MESH)
-    copy.start()
-    copies.append(copy)
+        copies.append(send(packed_ref, obs_ref.at[pl.ds(pl.multiple_of(seg * steps, steps), steps)],
+                           o_send.at[d], o_recv.at[d], {"tm": lax.rem(seg + d, segments)}))
+    copies.append(send(dyn_ref, full_ref.at[pl.ds(own_start, rows)], c_send, c_recv, {"state": near}))
     full_ref[pl.ds(own_start, rows)] = dyn_ref[...]
     obs_ref[pl.ds(pl.multiple_of(seg * steps, steps), steps)] = packed_ref[...]
     for i in range(PIECES):
         crossing[i].wait_recv()
-        spot = pl.ds(far_start + i * piece, piece)
-        copy = pltpu.make_async_remote_copy(
-            src_ref=full_ref.at[spot], dst_ref=full_ref.at[spot],
-            send_sem=f_send.at[i], recv_sem=f_recv.at[i],
-            device_id={"state": near}, device_id_type=MESH)
-        copy.start()
-        copies.append(copy)
-    for copy in crossing:
+        spot = pl.ds(pl.multiple_of(far_start + mine + i * piece, piece), piece)
+        swapping.append(send(full_ref.at[spot], full_ref.at[spot], y_send.at[i], y_recv.at[i], {"tm": across}))
+        copies.append(send(full_ref.at[spot], full_ref.at[spot], f_send.at[i], f_recv.at[i], {"state": near}))
+    for i in range(PIECES):
+        swapping[i].wait_recv()
+        spot = pl.ds(pl.multiple_of(far_start + theirs + i * piece, piece), piece)
+        copies.append(send(full_ref.at[spot], full_ref.at[spot], f_send.at[PIECES + i],
+                           f_recv.at[PIECES + i], {"state": near}))
+    for copy in crossing + swapping:
         copy.wait_send()
     for copy in copies:
         copy.wait()
@@ -99,7 +107,7 @@
 
 def compute_kernel(steps, full_ref, pattern_ref, mean_ref, obs_ref, filt_ref, smooth_ref,
                    power_hi, power_lo, powert_hi, powert_lo, r_hi, r_lo, p_hi, p_lo, h_hi, h_lo,
-                   scaled_ref, obs_in_ref, hr_hi, hr_lo, u_ref, v_ref, x_ref, own_x, own_p):
+                   scaled_ref, obs_in_ref, hr_hi, hr_lo, hrt_hi, hrt_lo, pt_hi, pt_lo, u_ref, v_ref, x_ref, own_x, own_p):
     width = full_ref.shape[1]
     total = obs_ref.shape[0]
     blocks = pattern_ref.shape[0]
@@ -166,9 +174,13 @@
         r_pair = halves(r_now)
         r_hi[levels, here, :], r_lo[levels, here, :] = r_pair
         p_hi[levels, here, :], p_lo[levels, here, :] = halves(p_now)
+        tall_here = pl.ds(pl.multiple_of(g * width, width), width)
+        pt_hi[tall_here, :], pt_lo[tall_here, :] = halves(p_now.T)
         pair = halves(inverse)
         h_hi[here, :], h_lo[here, :] = pair
-        hr_hi[here, :], hr_lo[here, :] = halves(multiply(pair, r_pair))
+        response = multiply(pair, r_pair)
+        hr_hi[here, :], hr_lo[here, :] = halves(response)
+        hrt_hi[tall_here, :], hrt_lo[tall_here, :] = halves(response.T)
         source = multiply(pair, halves(jnp.where(col == member, observed * root, 0.0)))
         obs_in_ref[here, :] = jnp.broadcast_to(
             jnp.sum(source.T, axis=0, keepdims=True), (group, group))
@@ -192,7 +204,8 @@
         here, small, spot = here_of(c)
         x_ref[pl.ds(pl.multiple_of(c * 8, 8), 8), :] = state
         first = pl.ds(pl.multiple_of((c // per_group) * group, group), 8)
-        drive = obs_in_ref[first, :] - few_rows(state, (hr_hi[here, :], hr_lo[here, :]), TRANS)
+        tall_here = pl.ds(pl.multiple_of((c // per_group) * width, width), width)
+        drive = obs_in_ref[first, :] - few_rows(state, (hrt_hi[tall_here, :], hrt_lo[tall_here, :]))
         drive = jnp.where(lane8 // steps == spot, drive, 0.0)
         u_ref[small, :] = u_ref[small, :] + drive
         return few_rows(state, top_t) + few_rows(drive, (p_hi[levels, here, :], p_lo[levels, here, :]))
@@ -212,12 +225,11 @@
         c = chunks - 1 - i
         here, small, spot = here_of(c)
         own_p[pl.ds(pl.multiple_of(c * 8, 8), 8), :] = state
-        seen = u_ref[small, :] - few_rows(state, (p_hi[levels, here, :], p_lo[levels, here, :]), TRANS)
+        tall_here = pl.ds(pl.multiple_of((c // per_group) * width, width), width)
+        seen = u_ref[small, :] - few_rows(state, (pt_hi[tall_here, :], pt_lo[tall_here, :]))
         seen = jnp.where(lane8 // steps == spot, seen, 0.0)
-        drive = few_rows(seen, (h_hi[here, :], h_lo[here, :]))
-        drive = jnp.where(lane8 // steps == spot, drive, 0.0)
-        v_ref[small, :] = v_ref[small, :] + drive
-        return few_rows(state, top) + few_rows(drive, (r_hi[levels, here, :], r_lo[levels, here, :]))
+        v_ref[small, :] = v_ref[small, :] + seen
+        return few_rows(state, top) + few_rows(seen, (hr_hi[here, :], hr_lo[here, :]))
 
     state = jnp.zeros((8, width), jnp.float32)
     if chunks <= 8:
@@ -233,7 +245,7 @@
     local = lane - spot * steps
     mine = (local >= 0) & (local < steps)
     u_own = jnp.where(mine, jnp.broadcast_to(u_ref[small, :][:1], (steps, group)), 0.0)
-    v_own = jnp.where(mine, jnp.broadcast_to(v_ref[small, :][:1], (steps, group)), 0.0)
+    v_own = jnp.where(mine, jnp.broadcast_to(few_rows(v_ref[small, :], (h_hi[here, :], h_lo[here, :]))[:1], (steps, group)), 0.0)
     enter = x_ref[pl.ds(pl.multiple_of(segment * 8, 8), 8), :][:1]
     leave = x_ref[pl.ds(pl.multiple_of((segment + 1) * 8, 8), 8), :][:1]
     after = own_p[pl.ds(pl.multiple_of(segment * 8, 8), 8), :][:1]
@@ -252,13 +264,14 @@
     xs = jnp.where(tall == steps - 1, jnp.broadcast_to(leave, (steps, width)), pltpu.roll(xs, steps - 1, 0))
     hits = scaled_ref[pl.ds(pl.multiple_of(segment * steps, steps), steps), :]
     change = jnp.sum(jnp.where(local == tau, v_own - u_own, 0.0), axis=1, keepdims=True)
-    filt_ref[...] = xs
-    smooth_ref[...] = xs + ps + hits * change
+    ss = xs + ps + hits * change
+    for i in range(steps):
+        filt_ref[i] = xs[i:i + 1]
+        smooth_ref[i] = ss[i:i + 1]
 
 
 def per_device(dynamics, pattern, initial_mean, observed, obs_index, obs_noise):
     rows, width = dynamics.shape
-    sequences = initial_mean.shape[0]
     steps = observed.shape[0]
     members = lax.axis_size("state")
     segments = lax.axis_size("tm")
@@ -266,24 +279,23 @@
     levels = steps.bit_length() - 1
     groups = total // LANES
     chunks = segments
-    packed = jnp.concatenate(
-        [observed, obs_index.astype(jnp.float32)[:, None], obs_noise[:, None],
-         jnp.zeros((steps, LANES - sequences - 2), jnp.float32)], axis=1)
     vmem = pl.BlockSpec(memory_space=pltpu.VMEM)
     dma = pltpu.SemaphoreType.DMA
     full, gathered = pl.pallas_call(
         functools.partial(gather_kernel, members, segments),
         out_shape=(jax.ShapeDtypeStruct((rows * members, width), jnp.float32),
                    jax.ShapeDtypeStruct((total, LANES), jnp.float32)),
-        in_specs=[vmem, vmem],
+        in_specs=[vmem] * 4,
         out_specs=(vmem, vmem),
-        scratch_shapes=[dma((PIECES,)), dma((PIECES,)), dma, dma, dma((PIECES,)), dma((PIECES,)),
+        scratch_shapes=[pltpu.VMEM((LANES, LANES), jnp.float32), pltpu.VMEM((steps, LANES), jnp.float32),
+                        dma((PIECES,)), dma((PIECES,)), dma((PIECES,)), dma((PIECES,)), dma, dma,
+                        dma((2 * PIECES,)), dma((2 * PIECES,)),
                         dma((segments,)), dma((segments,))],
         compiler_params=pltpu.CompilerParams(collective_id=0, has_side_effects=True),
         name="gather",
-    )(dynamics, packed)
+    )(dynamics, observed.T, obs_index[None, :], obs_noise[None, :])
     bf, f32 = jnp.bfloat16, jnp.float32
-    out = jax.ShapeDtypeStruct((steps, width), f32)
+    out = jax.ShapeDtypeStruct((steps, 1, width), f32)
     filtered, smoothed = pl.pallas_call(
         functools.partial(compute_kernel, steps),
         out_shape=(out, out),
@@ -295,12 +307,13 @@
             + [pltpu.VMEM((total, LANES), bf)] * 2
             + [pltpu.VMEM((total, width), f32), pltpu.VMEM((total, LANES), f32)]
             + [pltpu.VMEM((total, width), bf)] * 2
+            + [pltpu.VMEM((groups * width, LANES), bf)] * 4
             + [pltpu.VMEM((8 * groups, LANES), f32)] * 2
             + [pltpu.VMEM((8 * (chunks + 1), width), f32)] * 3),
         compiler_params=pltpu.CompilerParams(vmem_limit_bytes=56 * 1024 * 1024),
         name="smooth",
     )(full, pattern, initial_mean, gathered)
-    return filtered[:, None, :], smoothed[:, None, :]
+    return filtered, smoothed
 
 
 def solution(mesh):

time: 40.8 us -> 33.3 us (0.82)
  local copies, waits for them, and re-layouts: 4.21 us -> 0 us
  Pallas kernels: 35 us -> 32.5 us
  other arithmetic: 0.68 us -> 0 us
    unnamed x11 -> x0, local copies, waits for them, and re-layouts: 3.97 us -> none
    pallas_call x1, Pallas kernels: 18.3 us -> 16.1 us  [per_device(): pl.pallas_call(functools.partial(compute_kernel, steps), out_shape=(out,...]
    concatenate x1 -> x0, other arithmetic: 0.68 us -> none  [per_device(): jnp.concatenate([observed, obs_index.astype(jnp.float32)[:, None], obs_no...]
where the time goes in v2:
time: 33.3 us; the launch traced here: 33.2 us
  Pallas kernels  32.5 us (98%)
  between operations  0.64 us (2%)
    pallas_call x1, Pallas kernels, per_device(): pl.pallas_call(functools.partial(gather_kernel, members, segments), out_s...  16.4 us
    pallas_call x1, Pallas kernels, per_device(): pl.pallas_call(functools.partial(compute_kernel, steps), out_shape=(out,...  16.1 us

profile of v2, /device:TPU:0, one launch (start us, length us, event | category | flops | bytes accessed | tf_op | source)
XLA Modules:
  0.0 33.2 jit_solution(4412040541739528325)
XLA Ops:
  0.6 16.4 %gather.1 = (f32[512,512]{1,0:T(8,128)}, f32[128,128]{1,0:T(8,128)}) custom-call(f32[128,512]{1,0:T(8,128)} %dyn_ref.1, f32[4,16]{1,0:T(4,128)} %bitcast.3, s32[1,16]{1,0:T(1,128)} %bitcast.4, f32[1,16]{1,0:T(1,128)} %bitcast.5), custom_call_target="tpu_custom_call" | custom-call | tf_op jit(solution)/shard_map/gather/pallas_call | solution.py:284
  17.1 16.1 %smooth.1 = (f32[16,1,512]{2,1,0:T(1,128)}, f32[16,1,512]{2,1,0:T(1,128)}) custom-call(f32[512,512]{1,0:T(8,128)} %get-tuple-element.4.full_ref, s32[4,4]{1,0:T(4,128)} %pattern_ref.1, f32[4,512]{1,0:T(4,128)} %mean_ref.1, f32[128,128]{1,0:T(8,128)} %get-tuple-element.5.obs_ref), custom_call_target="tpu_custom_call" | custom-call | tf_op jit(solution)/shard_map/smooth/pallas_call | solution.py:299

commit v3 on v2

--- a/solution.py
+++ b/solution.py
@@ -14,7 +14,7 @@
 
 def gather_kernel(members, segments, dyn_ref, observed_ref, index_ref, noise_ref, full_ref, obs_ref,
                   raw_ref, packed_ref, x_send, x_recv, y_send, y_recv, c_send, c_recv,
-                  f_send, f_recv, o_send, o_recv):
+                  f_send, f_recv, o_send, o_recv, own_sem):
     me = lax.axis_index("state")
     seg = lax.axis_index("tm")
     rows = dyn_ref.shape[0]
@@ -61,7 +61,8 @@
         copies.append(send(packed_ref, obs_ref.at[pl.ds(pl.multiple_of(seg * steps, steps), steps)],
                            o_send.at[d], o_recv.at[d], {"tm": lax.rem(seg + d, segments)}))
     copies.append(send(dyn_ref, full_ref.at[pl.ds(own_start, rows)], c_send, c_recv, {"state": near}))
-    full_ref[pl.ds(own_start, rows)] = dyn_ref[...]
+    own_copy = pltpu.make_async_copy(dyn_ref, full_ref.at[pl.ds(own_start, rows)], own_sem)
+    own_copy.start()
     obs_ref[pl.ds(pl.multiple_of(seg * steps, steps), steps)] = packed_ref[...]
     for i in range(PIECES):
         crossing[i].wait_recv()
@@ -73,6 +74,7 @@
         spot = pl.ds(pl.multiple_of(far_start + theirs + i * piece, piece), piece)
         copies.append(send(full_ref.at[spot], full_ref.at[spot], f_send.at[PIECES + i],
                            f_recv.at[PIECES + i], {"state": near}))
+    own_copy.wait()
     for copy in crossing + swapping:
         copy.wait_send()
     for copy in copies:
@@ -90,8 +92,9 @@
 
 
 def multiply(left, right, dims=((1,), (0,))):
-    return (contract(left[0], right[1], dims) + contract(left[1], right[0], dims)) + contract(
-        left[0], right[0], dims)
+    stacked = jnp.concatenate([left[0], left[1], left[0]], axis=1)
+    other = jnp.concatenate([right[1], right[0], right[0]], axis=dims[1][0])
+    return contract(stacked, other, dims)
 
 
 TRANS = ((1,), (1,))
@@ -101,7 +104,7 @@
     count = left.shape[0]
     high = left.astype(jnp.bfloat16).astype(jnp.float32)
     both = jnp.concatenate([high, left - high], axis=0).astype(jnp.bfloat16)
-    total = contract(both, right[1], dims) + contract(both, right[0], dims)
+    total = contract(jnp.concatenate([both, both], axis=1), jnp.concatenate([right[1], right[0]], axis=dims[1][0]), dims)
     return total[:count] + total[count:]
 
 
@@ -126,16 +129,18 @@
             tile = full_ref[i * span:(i + 1) * span, j * span:(j + 1) * span]
             if i != j:
                 tile = tile * jnp.maximum(pattern_ref[i, j], 0).astype(jnp.float32)
-            hi, lo = halves(tile)
-            power_hi[0, i * span:(i + 1) * span, j * span:(j + 1) * span] = hi
-            power_lo[0, i * span:(i + 1) * span, j * span:(j + 1) * span] = lo
-
-    for k in range(levels):
+            down, over = slice(i * span, (i + 1) * span), slice(j * span, (j + 1) * span)
+            power_hi[0, down, over], power_lo[0, down, over] = halves(tile)
+            powert_hi[0, over, down], powert_lo[0, over, down] = halves(tile.T)
+
+    def advance(k):
         square = multiply((power_hi[k], power_lo[k]), (power_hi[k], power_lo[k]))
         power_hi[k + 1], power_lo[k + 1] = halves(square)
-    for k in range(levels + 1):
-        powert_hi[k] = power_hi[k].T
-        powert_lo[k] = power_lo[k].T
+        powert_hi[k + 1], powert_lo[k + 1] = halves(square.T)
+
+    if groups > 1:
+        for k in range(levels):
+            advance(k)
 
     row = lax.broadcasted_iota(jnp.int32, (group, group), 0)
     col = lax.broadcasted_iota(jnp.int32, (group, group), 1)
@@ -155,6 +160,8 @@
         r_now = multiply(halves(scaled), (power_hi[0], power_lo[0]))
         inverse = jnp.where(row == col, 1.0, 0.0)
         for k in range(levels):
+            if groups == 1:
+                advance(k)
             r_pair = halves(r_now)
             p_pair = halves(p_now)
             r_hi[k, here, :], r_lo[k, here, :] = r_pair
@@ -231,13 +238,6 @@
         v_ref[small, :] = v_ref[small, :] + seen
         return few_rows(state, top) + few_rows(seen, (hr_hi[here, :], hr_lo[here, :]))
 
-    state = jnp.zeros((8, width), jnp.float32)
-    if chunks <= 8:
-        for i in range(chunks):
-            state = backward(i, state)
-    else:
-        state = lax.fori_loop(0, chunks, backward, state)
-
     here, small, spot = here_of(segment)
     lane = lax.broadcasted_iota(jnp.int32, (steps, group), 1)
     tau = lax.broadcasted_iota(jnp.int32, (steps, group), 0)
@@ -245,23 +245,42 @@
     local = lane - spot * steps
     mine = (local >= 0) & (local < steps)
     u_own = jnp.where(mine, jnp.broadcast_to(u_ref[small, :][:1], (steps, group)), 0.0)
-    v_own = jnp.where(mine, jnp.broadcast_to(few_rows(v_ref[small, :], (h_hi[here, :], h_lo[here, :]))[:1], (steps, group)), 0.0)
     enter = x_ref[pl.ds(pl.multiple_of(segment * 8, 8), 8), :][:1]
     leave = x_ref[pl.ds(pl.multiple_of((segment + 1) * 8, 8), 8), :][:1]
+    first_xs = jnp.where(tall == 0, jnp.broadcast_to(enter, (steps, width)), 0.0)
+
+    def expand(k, xs):
+        size = 2**k
+        u_use = jnp.where((local >= tau - size) & (local < tau), u_own, 0.0)
+        moved = few_rows(pltpu.roll(xs, size, 0), (powert_hi[k], powert_lo[k])) + few_rows(
+            u_use, (p_hi[k, here, :], p_lo[k, here, :]))
+        return jnp.where(tall % (2 * size) == size, moved, xs)
+
+    state = jnp.zeros((8, width), jnp.float32)
+    xs = first_xs
+    if chunks <= 8:
+        for i in range(chunks):
+            state = backward(i, state)
+            if i < levels:
+                xs = expand(levels - 1 - i, xs)
+        done = min(chunks, levels)
+    else:
+        state = lax.fori_loop(0, chunks, backward, state)
+        done = 0
+    for i in range(done, levels):
+        xs = expand(levels - 1 - i, xs)
+    xs = jnp.where(tall == steps - 1, jnp.broadcast_to(leave, (steps, width)), pltpu.roll(xs, steps - 1, 0))
+
+    v_all = few_rows(v_ref[small, :], (h_hi[here, :], h_lo[here, :]))
+    v_own = jnp.where(mine, jnp.broadcast_to(v_all[:1], (steps, group)), 0.0)
     after = own_p[pl.ds(pl.multiple_of(segment * 8, 8), 8), :][:1]
-    xs = jnp.where(tall == 0, jnp.broadcast_to(enter, (steps, width)), 0.0)
     ps = jnp.where(tall == steps - 1, jnp.broadcast_to(after, (steps, width)), 0.0)
     for k in reversed(range(levels)):
         size = 2**k
-        u_use = jnp.where((local >= tau - size) & (local < tau), u_own, 0.0)
         v_use = jnp.where((local > tau) & (local <= tau + size), v_own, 0.0)
-        p_level = (p_hi[k, here, :], p_lo[k, here, :])
-        r_level = (r_hi[k, here, :], r_lo[k, here, :])
-        moved = few_rows(pltpu.roll(xs, size, 0), (powert_hi[k], powert_lo[k])) + few_rows(u_use, p_level)
-        xs = jnp.where(tall % (2 * size) == size, moved, xs)
-        moved = few_rows(pltpu.roll(ps, steps - size, 0), (power_hi[k], power_lo[k])) + few_rows(v_use, r_level)
+        moved = few_rows(pltpu.roll(ps, steps - size, 0), (power_hi[k], power_lo[k])) + few_rows(
+            v_use, (r_hi[k, here, :], r_lo[k, here, :]))
         ps = jnp.where((tall + 1) % (2 * size) == size, moved, ps)
-    xs = jnp.where(tall == steps - 1, jnp.broadcast_to(leave, (steps, width)), pltpu.roll(xs, steps - 1, 0))
     hits = scaled_ref[pl.ds(pl.multiple_of(segment * steps, steps), steps), :]
     change = jnp.sum(jnp.where(local == tau, v_own - u_own, 0.0), axis=1, keepdims=True)
     ss = xs + ps + hits * change
@@ -280,17 +299,18 @@
     groups = total // LANES
     chunks = segments
     vmem = pl.BlockSpec(memory_space=pltpu.VMEM)
+    hbm = pl.BlockSpec(memory_space=pl.ANY)
     dma = pltpu.SemaphoreType.DMA
     full, gathered = pl.pallas_call(
         functools.partial(gather_kernel, members, segments),
         out_shape=(jax.ShapeDtypeStruct((rows * members, width), jnp.float32),
                    jax.ShapeDtypeStruct((total, LANES), jnp.float32)),
-        in_specs=[vmem] * 4,
-        out_specs=(vmem, vmem),
+        in_specs=[hbm, vmem, vmem, vmem],
+        out_specs=(hbm, vmem),
         scratch_shapes=[pltpu.VMEM((LANES, LANES), jnp.float32), pltpu.VMEM((steps, LANES), jnp.float32),
                         dma((PIECES,)), dma((PIECES,)), dma((PIECES,)), dma((PIECES,)), dma, dma,
                         dma((2 * PIECES,)), dma((2 * PIECES,)),
-                        dma((segments,)), dma((segments,))],
+                        dma((segments,)), dma((segments,)), dma],
         compiler_params=pltpu.CompilerParams(collective_id=0, has_side_effects=True),
         name="gather",
     )(dynamics, observed.T, obs_index[None, :], obs_noise[None, :])

time: 33.3 us -> 33.2 us (level)
    pallas_call x1, Pallas kernels: 16.1 us -> 15.5 us  [per_device(): pl.pallas_call(functools.partial(compute_kernel, steps), out_shape=(out,...]
    pallas_call x1, Pallas kernels: 16.4 us -> 16.9 us  [per_device(): pl.pallas_call(functools.partial(gather_kernel, members, segments), out_s...]
where the time goes in v3:
time: 33.2 us; the launch traced here: 33 us
  Pallas kernels  32.4 us (98%)
  between operations  0.64 us (2%)
    pallas_call x1, Pallas kernels, per_device(): pl.pallas_call(functools.partial(gather_kernel, members, segments), out_s...  16.9 us
    pallas_call x1, Pallas kernels, per_device(): pl.pallas_call(functools.partial(compute_kernel, steps), out_shape=(out,...  15.5 us

profile of v3, /device:TPU:0, one launch (start us, length us, event | category | flops | bytes accessed | tf_op | source)
XLA Modules:
  0.0 33.0 jit_solution(13534684984536661785)
XLA Ops:
  0.6 16.9 %gather.1 = (f32[512,512]{1,0:T(8,128)}, f32[128,128]{1,0:T(8,128)}) custom-call(f32[128,512]{1,0:T(8,128)} %dyn_ref.1, f32[4,16]{1,0:T(4,128)} %bitcast.3, s32[1,16]{1,0:T(1,128)} %bitcast.4, f32[1,16]{1,0:T(1,128)} %bitcast.5), custom_call_target="tpu_custom_call" | custom-call | tf_op jit(solution)/shard_map/gather/pallas_call | solution.py:304
  17.5 15.5 %smooth.1 = (f32[16,1,512]{2,1,0:T(1,128)}, f32[16,1,512]{2,1,0:T(1,128)}) custom-call(f32[512,512]{1,0:T(8,128)} %get-tuple-element.4.full_ref, s32[4,4]{1,0:T(4,128)} %pattern_ref.1, f32[4,512]{1,0:T(4,128)} %mean_ref.1, f32[128,128]{1,0:T(8,128)} %get-tuple-element.5.obs_ref), custom_call_target="tpu_custom_call" | custom-call | tf_op jit(solution)/shard_map/smooth/pallas_call | solution.py:319

commit v4 on v3

--- a/solution.py
+++ b/solution.py
@@ -28,11 +28,6 @@
     pl.semaphore_signal(barrier, inc=1, device_id={"state": near}, device_id_type=MESH)
     for d in range(1, segments):
         pl.semaphore_signal(barrier, inc=1, device_id={"tm": lax.rem(seg + d, segments)}, device_id_type=MESH)
-    raw_ref[...] = jnp.zeros_like(raw_ref)
-    raw_ref[:sequences, :steps] = observed_ref[...]
-    raw_ref[sequences:sequences + 1, :steps] = index_ref[...].astype(jnp.float32)
-    raw_ref[sequences + 1:sequences + 2, :steps] = noise_ref[...]
-    packed_ref[...] = raw_ref[...].T[:steps]
     pl.semaphore_wait(barrier, segments + 1)
 
     half = rows // 2
@@ -57,10 +52,15 @@
         crossing.append(send(dyn_ref.at[pl.ds(at, piece)],
                              full_ref.at[pl.ds(pl.multiple_of(own_start + at, piece), piece)],
                              x_send.at[i], x_recv.at[i], {"state": far}))
+    copies.append(send(dyn_ref, full_ref.at[pl.ds(own_start, rows)], c_send, c_recv, {"state": near}))
+    raw_ref[...] = jnp.zeros_like(raw_ref)
+    raw_ref[:sequences, :steps] = observed_ref[...]
+    raw_ref[sequences:sequences + 1, :steps] = index_ref[...].astype(jnp.float32)
+    raw_ref[sequences + 1:sequences + 2, :steps] = noise_ref[...]
+    packed_ref[...] = raw_ref[...].T[:steps]
     for d in range(1, segments):
         copies.append(send(packed_ref, obs_ref.at[pl.ds(pl.multiple_of(seg * steps, steps), steps)],
                            o_send.at[d], o_recv.at[d], {"tm": lax.rem(seg + d, segments)}))
-    copies.append(send(dyn_ref, full_ref.at[pl.ds(own_start, rows)], c_send, c_recv, {"state": near}))
     own_copy = pltpu.make_async_copy(dyn_ref, full_ref.at[pl.ds(own_start, rows)], own_sem)
     own_copy.start()
     obs_ref[pl.ds(pl.multiple_of(seg * steps, steps), steps)] = packed_ref[...]
@@ -110,7 +110,7 @@
 
 def compute_kernel(steps, full_ref, pattern_ref, mean_ref, obs_ref, filt_ref, smooth_ref,
                    power_hi, power_lo, powert_hi, powert_lo, r_hi, r_lo, p_hi, p_lo, h_hi, h_lo,
-                   scaled_ref, obs_in_ref, hr_hi, hr_lo, hrt_hi, hrt_lo, pt_hi, pt_lo, u_ref, v_ref, x_ref, own_x, own_p):
+                   scaled_ref, obs_in_ref, hr_hi, hr_lo, hrt_hi, hrt_lo, pt_hi, pt_lo, th_hi, th_lo, tp_hi, tp_lo, kt_hi, kt_lo, kb_hi, kb_lo, u_ref, v_ref, x_ref, own_x, own_p):
     width = full_ref.shape[1]
     total = obs_ref.shape[0]
     blocks = pattern_ref.shape[0]
@@ -188,6 +188,16 @@
         response = multiply(pair, r_pair)
         hr_hi[here, :], hr_lo[here, :] = halves(response)
         hrt_hi[tall_here, :], hrt_lo[tall_here, :] = halves(response.T)
+        if groups == 1:
+            p_pair = halves(p_now)
+            response_pair = halves(response)
+            th_hi[...], th_lo[...] = halves(
+                multiply(response_pair, (power_hi[levels], power_lo[levels])).T)
+            tp_hi[...], tp_lo[...] = halves(
+                multiply(p_pair, (powert_hi[levels], powert_lo[levels])).T)
+            link = multiply(p_pair, response_pair, TRANS)
+            kt_hi[...], kt_lo[...] = halves(link)
+            kb_hi[...], kb_lo[...] = halves(link.T)
         source = multiply(pair, halves(jnp.where(col == member, observed * root, 0.0)))
         obs_in_ref[here, :] = jnp.broadcast_to(
             jnp.sum(source.T, axis=0, keepdims=True), (group, group))
@@ -221,9 +231,21 @@
         jnp.where(lax.broadcasted_iota(jnp.int32, mean_ref.shape, 0) == member, mean_ref[...], 0.0),
         axis=0, keepdims=True)
     state = jnp.broadcast_to(mean, (8, width))
-    if chunks <= 8:
+    ahead = groups == 1 and chunks <= 8
+    if ahead:
+        th, tp = (th_hi[...], th_lo[...]), (tp_hi[...], tp_lo[...])
+        kt, kb = (kt_hi[...], kt_lo[...]), (kb_hi[...], kb_lo[...])
+        base = obs_in_ref[:8, :]
+        shown = few_rows(state, (hrt_hi[...], hrt_lo[...]))
+        every = jnp.zeros((8, group), jnp.float32)
         for c in range(chunks):
-            state = forward(c, state)
+            x_ref[c * 8:(c + 1) * 8, :] = state
+            drive = jnp.where(lane8 // steps == c, base - shown, 0.0)
+            every = every + drive
+            if c + 1 < chunks:
+                shown = few_rows(state, th) + few_rows(drive, kt)
+            state = few_rows(state, top_t) + few_rows(drive, (p_hi[levels], p_lo[levels]))
+        u_ref[...] = every
     else:
         state = lax.fori_loop(0, chunks, forward, state)
     x_ref[chunks * 8:(chunks + 1) * 8, :] = state
@@ -258,11 +280,27 @@
 
     state = jnp.zeros((8, width), jnp.float32)
     xs = first_xs
-    if chunks <= 8:
+    if ahead:
+        known = every
+        shown = jnp.zeros((8, group), jnp.float32)
+        every = jnp.zeros((8, group), jnp.float32)
         for i in range(chunks):
-            state = backward(i, state)
+            c = chunks - 1 - i
+            own_p[c * 8:(c + 1) * 8, :] = state
+            seen = jnp.where(lane8 // steps == c, known - shown, 0.0)
+            every = every + seen
+            if c > 0:
+                pushed = few_rows(seen, kb)
+                if i > 0:
+                    pushed = pushed + few_rows(state, tp)
+                shown = pushed
+                moved = few_rows(seen, (hr_hi[...], hr_lo[...]))
+                if i > 0:
+                    moved = moved + few_rows(state, top)
+                state = moved
             if i < levels:
                 xs = expand(levels - 1 - i, xs)
+        v_ref[...] = every
         done = min(chunks, levels)
     else:
         state = lax.fori_loop(0, chunks, backward, state)
@@ -306,7 +344,7 @@
         out_shape=(jax.ShapeDtypeStruct((rows * members, width), jnp.float32),
                    jax.ShapeDtypeStruct((total, LANES), jnp.float32)),
         in_specs=[hbm, vmem, vmem, vmem],
-        out_specs=(hbm, vmem),
+        out_specs=(vmem, vmem),
         scratch_shapes=[pltpu.VMEM((LANES, LANES), jnp.float32), pltpu.VMEM((steps, LANES), jnp.float32),
                         dma((PIECES,)), dma((PIECES,)), dma((PIECES,)), dma((PIECES,)), dma, dma,
                         dma((2 * PIECES,)), dma((2 * PIECES,)),
@@ -328,6 +366,8 @@
             + [pltpu.VMEM((total, width), f32), pltpu.VMEM((total, LANES), f32)]
             + [pltpu.VMEM((total, width), bf)] * 2
             + [pltpu.VMEM((groups * width, LANES), bf)] * 4
+            + [pltpu.VMEM((width, LANES), bf)] * 4
+            + [pltpu.VMEM((LANES, LANES), bf)] * 4
             + [pltpu.VMEM((8 * groups, LANES), f32)] * 2
             + [pltpu.VMEM((8 * (chunks + 1), width), f32)] * 3),
         compiler_params=pltpu.CompilerParams(vmem_limit_bytes=56 * 1024 * 1024),

time: 33.2 us -> 33.2 us (level)
    pallas_call x1, Pallas kernels: 16.9 us -> 16.4 us  [per_device(): pl.pallas_call(functools.partial(gather_kernel, members, segments), out_s...]
    pallas_call x1, Pallas kernels: 15.5 us -> 16 us  [per_device(): pl.pallas_call(functools.partial(compute_kernel, steps), out_shape=(out,...]
where the time goes in v4:
time: 33.2 us; the launch traced here: 33 us
  Pallas kernels  32.4 us (98%)
  between operations  0.64 us (2%)
    pallas_call x1, Pallas kernels, per_device(): pl.pallas_call(functools.partial(gather_kernel, members, segments), out_s...  16.4 us
    pallas_call x1, Pallas kernels, per_device(): pl.pallas_call(functools.partial(compute_kernel, steps), out_shape=(out,...  16 us

profile of v4, /device:TPU:0, one launch (start us, length us, event | category | flops | bytes accessed | tf_op | source)
XLA Modules:
  0.0 33.0 jit_solution(7369292145008651901)
XLA Ops:
  0.6 16.4 %gather.1 = (f32[512,512]{1,0:T(8,128)}, f32[128,128]{1,0:T(8,128)}) custom-call(f32[128,512]{1,0:T(8,128)} %dyn_ref.1, f32[4,16]{1,0:T(4,128)} %bitcast.3, s32[1,16]{1,0:T(1,128)} %bitcast.4, f32[1,16]{1,0:T(1,128)} %bitcast.5), custom_call_target="tpu_custom_call" | custom-call | tf_op jit(solution)/shard_map/gather/pallas_call | solution.py:342
  17.0 16.0 %smooth.1 = (f32[16,1,512]{2,1,0:T(1,128)}, f32[16,1,512]{2,1,0:T(1,128)}) custom-call(f32[512,512]{1,0:T(8,128)} %get-tuple-element.4.full_ref, s32[4,4]{1,0:T(4,128)} %pattern_ref.1, f32[4,512]{1,0:T(4,128)} %mean_ref.1, f32[128,128]{1,0:T(8,128)} %get-tuple-element.5.obs_ref), custom_call_target="tpu_custom_call" | custom-call | tf_op jit(solution)/shard_map/smooth/pallas_call | solution.py:357

commit v5 on v3

--- a/solution.py
+++ b/solution.py
@@ -28,11 +28,6 @@
     pl.semaphore_signal(barrier, inc=1, device_id={"state": near}, device_id_type=MESH)
     for d in range(1, segments):
         pl.semaphore_signal(barrier, inc=1, device_id={"tm": lax.rem(seg + d, segments)}, device_id_type=MESH)
-    raw_ref[...] = jnp.zeros_like(raw_ref)
-    raw_ref[:sequences, :steps] = observed_ref[...]
-    raw_ref[sequences:sequences + 1, :steps] = index_ref[...].astype(jnp.float32)
-    raw_ref[sequences + 1:sequences + 2, :steps] = noise_ref[...]
-    packed_ref[...] = raw_ref[...].T[:steps]
     pl.semaphore_wait(barrier, segments + 1)
 
     half = rows // 2
@@ -57,10 +52,15 @@
         crossing.append(send(dyn_ref.at[pl.ds(at, piece)],
                              full_ref.at[pl.ds(pl.multiple_of(own_start + at, piece), piece)],
                              x_send.at[i], x_recv.at[i], {"state": far}))
+    copies.append(send(dyn_ref, full_ref.at[pl.ds(own_start, rows)], c_send, c_recv, {"state": near}))
+    raw_ref[...] = jnp.zeros_like(raw_ref)
+    raw_ref[:sequences, :steps] = observed_ref[...]
+    raw_ref[sequences:sequences + 1, :steps] = index_ref[...].astype(jnp.float32)
+    raw_ref[sequences + 1:sequences + 2, :steps] = noise_ref[...]
+    packed_ref[...] = raw_ref[...].T[:steps]
     for d in range(1, segments):
         copies.append(send(packed_ref, obs_ref.at[pl.ds(pl.multiple_of(seg * steps, steps), steps)],
                            o_send.at[d], o_recv.at[d], {"tm": lax.rem(seg + d, segments)}))
-    copies.append(send(dyn_ref, full_ref.at[pl.ds(own_start, rows)], c_send, c_recv, {"state": near}))
     own_copy = pltpu.make_async_copy(dyn_ref, full_ref.at[pl.ds(own_start, rows)], own_sem)
     own_copy.start()
     obs_ref[pl.ds(pl.multiple_of(seg * steps, steps), steps)] = packed_ref[...]
@@ -97,20 +97,30 @@
     return contract(stacked, other, dims)
 
 
+def stacked_left(pair):
+    return jnp.concatenate([pair[0], pair[1], pair[0]], axis=1)
+
+
+def keep_rows(ref, index, start, pair, times):
+    size = pair[0].shape[0]
+    for i, part in enumerate((pair[1], pair[0], pair[0])[:times]):
+        ref[index + (pl.ds(pl.multiple_of(start + i * size, size), size), slice(None))] = part
+
+
 TRANS = ((1,), (1,))
 
 
-def few_rows(left, right, dims=((1,), (0,))):
+def few_rows(left, right):
     count = left.shape[0]
     high = left.astype(jnp.bfloat16).astype(jnp.float32)
     both = jnp.concatenate([high, left - high], axis=0).astype(jnp.bfloat16)
-    total = contract(jnp.concatenate([both, both], axis=1), jnp.concatenate([right[1], right[0]], axis=dims[1][0]), dims)
+    total = contract(jnp.concatenate([both, both], axis=1), right, ((1,), (0,)))
     return total[:count] + total[count:]
 
 
 def compute_kernel(steps, full_ref, pattern_ref, mean_ref, obs_ref, filt_ref, smooth_ref,
-                   power_hi, power_lo, powert_hi, powert_lo, r_hi, r_lo, p_hi, p_lo, h_hi, h_lo,
-                   scaled_ref, obs_in_ref, hr_hi, hr_lo, hrt_hi, hrt_lo, pt_hi, pt_lo, u_ref, v_ref, x_ref, own_x, own_p):
+                   power_left, power, power_t, r_rows, p_rows, h_rows, hr_rows, hr_t, p_t,
+                   scaled_ref, obs_in_ref, u_ref, v_ref, x_ref, own_x, own_p):
     width = full_ref.shape[1]
     total = obs_ref.shape[0]
     blocks = pattern_ref.shape[0]
@@ -130,13 +140,22 @@
             if i != j:
                 tile = tile * jnp.maximum(pattern_ref[i, j], 0).astype(jnp.float32)
             down, over = slice(i * span, (i + 1) * span), slice(j * span, (j + 1) * span)
-            power_hi[0, down, over], power_lo[0, down, over] = halves(tile)
-            powert_hi[0, over, down], powert_lo[0, over, down] = halves(tile.T)
+            hi, lo = halves(tile)
+            turned_hi, turned_lo = halves(tile.T)
+            for n, (part, turned) in enumerate(((lo, turned_lo), (hi, turned_hi), (hi, turned_hi))):
+                power[0, n * width + i * span:n * width + (i + 1) * span, over] = part
+                power_t[0, n * width + j * span:n * width + (j + 1) * span, down] = turned
+            for n, part in enumerate((hi, lo, hi)):
+                power_left[0, down, n * width + j * span:n * width + (j + 1) * span] = part
 
     def advance(k):
-        square = multiply((power_hi[k], power_lo[k]), (power_hi[k], power_lo[k]))
-        power_hi[k + 1], power_lo[k + 1] = halves(square)
-        powert_hi[k + 1], powert_lo[k + 1] = halves(square.T)
+        square = contract(power_left[k], power[k], ((1,), (0,)))
+        hi, lo = halves(square)
+        keep_rows(power, (k + 1,), 0, (hi, lo), 3)
+        keep_rows(power_t, (k + 1,), 0, halves(square.T), 3)
+        if k + 1 < levels:
+            for n, part in enumerate((hi, lo, hi)):
+                power_left[k + 1, :, n * width:(n + 1) * width] = part
 
     if groups > 1:
         for k in range(levels):
@@ -157,15 +176,16 @@
         scaled = jnp.where(wide == index, root, 0.0)
         scaled_ref[here, :] = scaled
         p_now = scaled
-        r_now = multiply(halves(scaled), (power_hi[0], power_lo[0]))
+        two = 2 * group * g
+        r_now = contract(stacked_left(halves(scaled)), power[0], ((1,), (0,)))
         inverse = jnp.where(row == col, 1.0, 0.0)
         for k in range(levels):
             if groups == 1:
                 advance(k)
             r_pair = halves(r_now)
             p_pair = halves(p_now)
-            r_hi[k, here, :], r_lo[k, here, :] = r_pair
-            p_hi[k, here, :], p_lo[k, here, :] = p_pair
+            keep_rows(r_rows, (k,), two, r_pair, 2)
+            keep_rows(p_rows, (k,), two, p_pair, 2)
             gram = multiply(r_pair, p_pair, TRANS)
             size = 2**k
             sibling = ((row // (2 * size)) == (col // (2 * size))) & ((row // size) == (col // size) + 1)
@@ -176,18 +196,17 @@
                 pair = halves(inverse)
                 inverse = inverse - multiply(halves(multiply(pair, halves(gram))), pair)
             set_bit = ((row_wide // size) % 2) == 1
-            r_now = jnp.where(set_bit, multiply(r_pair, (power_hi[k], power_lo[k])), r_now)
-            p_now = jnp.where(set_bit, p_now, multiply(p_pair, (powert_hi[k], powert_lo[k])))
+            r_now = jnp.where(set_bit, contract(stacked_left(r_pair), power[k], ((1,), (0,))), r_now)
+            p_now = jnp.where(set_bit, p_now, contract(stacked_left(p_pair), power_t[k], ((1,), (0,))))
         r_pair = halves(r_now)
-        r_hi[levels, here, :], r_lo[levels, here, :] = r_pair
-        p_hi[levels, here, :], p_lo[levels, here, :] = halves(p_now)
-        tall_here = pl.ds(pl.multiple_of(g * width, width), width)
-        pt_hi[tall_here, :], pt_lo[tall_here, :] = halves(p_now.T)
+        keep_rows(r_rows, (levels,), two, r_pair, 2)
+        keep_rows(p_rows, (levels,), two, halves(p_now), 2)
+        keep_rows(p_t, (), 2 * width * g, halves(p_now.T), 2)
         pair = halves(inverse)
-        h_hi[here, :], h_lo[here, :] = pair
+        keep_rows(h_rows, (), two, pair, 2)
         response = multiply(pair, r_pair)
-        hr_hi[here, :], hr_lo[here, :] = halves(response)
-        hrt_hi[tall_here, :], hrt_lo[tall_here, :] = halves(response.T)
+        keep_rows(hr_rows, (), two, halves(response), 2)
+        keep_rows(hr_t, (), 2 * width * g, halves(response.T), 2)
         source = multiply(pair, halves(jnp.where(col == member, observed * root, 0.0)))
         obs_in_ref[here, :] = jnp.broadcast_to(
             jnp.sum(source.T, axis=0, keepdims=True), (group, group))
@@ -200,22 +219,22 @@
     lane8 = lax.broadcasted_iota(jnp.int32, (8, group), 1)
     u_ref[...] = jnp.zeros_like(u_ref)
     v_ref[...] = jnp.zeros_like(v_ref)
-    top = (power_hi[levels], power_lo[levels])
-    top_t = (powert_hi[levels], powert_lo[levels])
+    top, top_t = power[levels, :2 * width], power_t[levels, :2 * width]
 
     def here_of(c):
         g = c // per_group
-        return pl.ds(pl.multiple_of(g * group, group), group), pl.ds(pl.multiple_of(g * 8, 8), 8), c % per_group
+        return (pl.ds(pl.multiple_of(g * 2 * group, 2 * group), 2 * group),
+                pl.ds(pl.multiple_of(g * 8, 8), 8), c % per_group,
+                pl.ds(pl.multiple_of(g * 2 * width, 2 * width), 2 * width))
 
     def forward(c, state):
-        here, small, spot = here_of(c)
+        here, small, spot, tall_here = here_of(c)
         x_ref[pl.ds(pl.multiple_of(c * 8, 8), 8), :] = state
         first = pl.ds(pl.multiple_of((c // per_group) * group, group), 8)
-        tall_here = pl.ds(pl.multiple_of((c // per_group) * width, width), width)
-        drive = obs_in_ref[first, :] - few_rows(state, (hrt_hi[tall_here, :], hrt_lo[tall_here, :]))
+        drive = obs_in_ref[first, :] - few_rows(state, hr_t[tall_here, :])
         drive = jnp.where(lane8 // steps == spot, drive, 0.0)
         u_ref[small, :] = u_ref[small, :] + drive
-        return few_rows(state, top_t) + few_rows(drive, (p_hi[levels, here, :], p_lo[levels, here, :]))
+        return few_rows(state, top_t) + few_rows(drive, p_rows[levels, here, :])
 
     mean = jnp.sum(
         jnp.where(lax.broadcasted_iota(jnp.int32, mean_ref.shape, 0) == member, mean_ref[...], 0.0),
@@ -230,15 +249,14 @@
 
     def backward(i, state):
         c = chunks - 1 - i
-        here, small, spot = here_of(c)
+        here, small, spot, tall_here = here_of(c)
         own_p[pl.ds(pl.multiple_of(c * 8, 8), 8), :] = state
-        tall_here = pl.ds(pl.multiple_of((c // per_group) * width, width), width)
-        seen = u_ref[small, :] - few_rows(state, (pt_hi[tall_here, :], pt_lo[tall_here, :]))
+        seen = u_ref[small, :] - few_rows(state, p_t[tall_here, :])
         seen = jnp.where(lane8 // steps == spot, seen, 0.0)
         v_ref[small, :] = v_ref[small, :] + seen
-        return few_rows(state, top) + few_rows(seen, (hr_hi[here, :], hr_lo[here, :]))
-
-    here, small, spot = here_of(segment)
+        return few_rows(state, top) + few_rows(seen, hr_rows[here, :])
+
+    here, small, spot, _ = here_of(segment)
     lane = lax.broadcasted_iota(jnp.int32, (steps, group), 1)
     tau = lax.broadcasted_iota(jnp.int32, (steps, group), 0)
     tall = lax.broadcasted_iota(jnp.int32, (steps, width), 0)
@@ -252,8 +270,8 @@
     def expand(k, xs):
         size = 2**k
         u_use = jnp.where((local >= tau - size) & (local < tau), u_own, 0.0)
-        moved = few_rows(pltpu.roll(xs, size, 0), (powert_hi[k], powert_lo[k])) + few_rows(
-            u_use, (p_hi[k, here, :], p_lo[k, here, :]))
+        moved = few_rows(pltpu.roll(xs, size, 0), power_t[k, :2 * width]) + few_rows(
+            u_use, p_rows[k, here, :])
         return jnp.where(tall % (2 * size) == size, moved, xs)
 
     state = jnp.zeros((8, width), jnp.float32)
@@ -271,15 +289,15 @@
         xs = expand(levels - 1 - i, xs)
     xs = jnp.where(tall == steps - 1, jnp.broadcast_to(leave, (steps, width)), pltpu.roll(xs, steps - 1, 0))
 
-    v_all = few_rows(v_ref[small, :], (h_hi[here, :], h_lo[here, :]))
+    v_all = few_rows(v_ref[small, :], h_rows[here, :])
     v_own = jnp.where(mine, jnp.broadcast_to(v_all[:1], (steps, group)), 0.0)
     after = own_p[pl.ds(pl.multiple_of(segment * 8, 8), 8), :][:1]
     ps = jnp.where(tall == steps - 1, jnp.broadcast_to(after, (steps, width)), 0.0)
     for k in reversed(range(levels)):
         size = 2**k
         v_use = jnp.where((local > tau) & (local <= tau + size), v_own, 0.0)
-        moved = few_rows(pltpu.roll(ps, steps - size, 0), (power_hi[k], power_lo[k])) + few_rows(
-            v_use, (r_hi[k, here, :], r_lo[k, here, :]))
+        moved = few_rows(pltpu.roll(ps, steps - size, 0), power[k, :2 * width]) + few_rows(
+            v_use, r_rows[k, here, :])
         ps = jnp.where((tall + 1) % (2 * size) == size, moved, ps)
     hits = scaled_ref[pl.ds(pl.multiple_of(segment * steps, steps), steps), :]
     change = jnp.sum(jnp.where(local == tau, v_own - u_own, 0.0), axis=1, keepdims=True)
@@ -306,7 +324,7 @@
         out_shape=(jax.ShapeDtypeStruct((rows * members, width), jnp.float32),
                    jax.ShapeDtypeStruct((total, LANES), jnp.float32)),
         in_specs=[hbm, vmem, vmem, vmem],
-        out_specs=(hbm, vmem),
+        out_specs=(vmem, vmem),
         scratch_shapes=[pltpu.VMEM((LANES, LANES), jnp.float32), pltpu.VMEM((steps, LANES), jnp.float32),
                         dma((PIECES,)), dma((PIECES,)), dma((PIECES,)), dma((PIECES,)), dma, dma,
                         dma((2 * PIECES,)), dma((2 * PIECES,)),
@@ -322,12 +340,12 @@
         in_specs=[vmem, pl.BlockSpec(memory_space=pltpu.SMEM), vmem, vmem],
         out_specs=(vmem, vmem),
         scratch_shapes=(
-            [pltpu.VMEM((levels + 1, width, width), bf)] * 4
-            + [pltpu.VMEM((levels + 1, total, width), bf)] * 4
-            + [pltpu.VMEM((total, LANES), bf)] * 2
+            [pltpu.VMEM((levels, width, 3 * width), bf)]
+            + [pltpu.VMEM((levels + 1, 3 * width, width), bf)] * 2
+            + [pltpu.VMEM((levels + 1, 2 * total, width), bf)] * 2
+            + [pltpu.VMEM((2 * total, LANES), bf), pltpu.VMEM((2 * total, width), bf)]
+            + [pltpu.VMEM((2 * groups * width, LANES), bf)] * 2
             + [pltpu.VMEM((total, width), f32), pltpu.VMEM((total, LANES), f32)]
-            + [pltpu.VMEM((total, width), bf)] * 2
-            + [pltpu.VMEM((groups * width, LANES), bf)] * 4
             + [pltpu.VMEM((8 * groups, LANES), f32)] * 2
             + [pltpu.VMEM((8 * (chunks + 1), width), f32)] * 3),
         compiler_params=pltpu.CompilerParams(vmem_limit_bytes=56 * 1024 * 1024),

time: 33.2 us -> 33.1 us (level)
    pallas_call x1, Pallas kernels: 16.9 us -> 16.4 us  [per_device(): pl.pallas_call(functools.partial(gather_kernel, members, segments), out_s...]
    pallas_call x1, Pallas kernels: 15.5 us -> 16 us  [per_device(): pl.pallas_call(functools.partial(compute_kernel, steps), out_shape=(out,...]
where the time goes in v5:
time: 33.1 us; the launch traced here: 33 us
  Pallas kernels  32.3 us (98%)
  between operations  0.64 us (2%)
    pallas_call x1, Pallas kernels, per_device(): pl.pallas_call(functools.partial(gather_kernel, members, segments), out_s...  16.4 us
    pallas_call x1, Pallas kernels, per_device(): pl.pallas_call(functools.partial(compute_kernel, steps), out_shape=(out,...  16 us

profile of v5, /device:TPU:0, one launch (start us, length us, event | category | flops | bytes accessed | tf_op | source)
XLA Modules:
  0.0 33.0 jit_solution(12813605389086038060)
XLA Ops:
  0.6 16.4 %gather.1 = (f32[512,512]{1,0:T(8,128)}, f32[128,128]{1,0:T(8,128)}) custom-call(f32[128,512]{1,0:T(8,128)} %dyn_ref.1, f32[4,16]{1,0:T(4,128)} %bitcast.3, s32[1,16]{1,0:T(1,128)} %bitcast.4, f32[1,16]{1,0:T(1,128)} %bitcast.5), custom_call_target="tpu_custom_call" | custom-call | tf_op jit(solution)/shard_map/gather/pallas_call | solution.py:322
  17.0 16.0 %smooth.1 = (f32[16,1,512]{2,1,0:T(1,128)}, f32[16,1,512]{2,1,0:T(1,128)}) custom-call(f32[512,512]{1,0:T(8,128)} %get-tuple-element.4.full_ref, s32[4,4]{1,0:T(4,128)} %pattern_ref.1, f32[4,512]{1,0:T(4,128)} %mean_ref.1, f32[128,128]{1,0:T(8,128)} %get-tuple-element.5.obs_ref), custom_call_target="tpu_custom_call" | custom-call | tf_op jit(solution)/shard_map/smooth/pallas_call | solution.py:337

commit v6 on v3

--- a/solution.py
+++ b/solution.py
@@ -28,11 +28,6 @@
     pl.semaphore_signal(barrier, inc=1, device_id={"state": near}, device_id_type=MESH)
     for d in range(1, segments):
         pl.semaphore_signal(barrier, inc=1, device_id={"tm": lax.rem(seg + d, segments)}, device_id_type=MESH)
-    raw_ref[...] = jnp.zeros_like(raw_ref)
-    raw_ref[:sequences, :steps] = observed_ref[...]
-    raw_ref[sequences:sequences + 1, :steps] = index_ref[...].astype(jnp.float32)
-    raw_ref[sequences + 1:sequences + 2, :steps] = noise_ref[...]
-    packed_ref[...] = raw_ref[...].T[:steps]
     pl.semaphore_wait(barrier, segments + 1)
 
     half = rows // 2
@@ -57,10 +52,15 @@
         crossing.append(send(dyn_ref.at[pl.ds(at, piece)],
                              full_ref.at[pl.ds(pl.multiple_of(own_start + at, piece), piece)],
                              x_send.at[i], x_recv.at[i], {"state": far}))
+    copies.append(send(dyn_ref, full_ref.at[pl.ds(own_start, rows)], c_send, c_recv, {"state": near}))
+    raw_ref[...] = jnp.zeros_like(raw_ref)
+    raw_ref[:sequences, :steps] = observed_ref[...]
+    raw_ref[sequences:sequences + 1, :steps] = index_ref[...].astype(jnp.float32)
+    raw_ref[sequences + 1:sequences + 2, :steps] = noise_ref[...]
+    packed_ref[...] = raw_ref[...].T[:steps]
     for d in range(1, segments):
         copies.append(send(packed_ref, obs_ref.at[pl.ds(pl.multiple_of(seg * steps, steps), steps)],
                            o_send.at[d], o_recv.at[d], {"tm": lax.rem(seg + d, segments)}))
-    copies.append(send(dyn_ref, full_ref.at[pl.ds(own_start, rows)], c_send, c_recv, {"state": near}))
     own_copy = pltpu.make_async_copy(dyn_ref, full_ref.at[pl.ds(own_start, rows)], own_sem)
     own_copy.start()
     obs_ref[pl.ds(pl.multiple_of(seg * steps, steps), steps)] = packed_ref[...]
@@ -306,12 +306,13 @@
         out_shape=(jax.ShapeDtypeStruct((rows * members, width), jnp.float32),
                    jax.ShapeDtypeStruct((total, LANES), jnp.float32)),
         in_specs=[hbm, vmem, vmem, vmem],
-        out_specs=(hbm, vmem),
+        out_specs=(vmem, vmem),
         scratch_shapes=[pltpu.VMEM((LANES, LANES), jnp.float32), pltpu.VMEM((steps, LANES), jnp.float32),
                         dma((PIECES,)), dma((PIECES,)), dma((PIECES,)), dma((PIECES,)), dma, dma,
                         dma((2 * PIECES,)), dma((2 * PIECES,)),
                         dma((segments,)), dma((segments,)), dma],
-        compiler_params=pltpu.CompilerParams(collective_id=0, has_side_effects=True),
+        compiler_params=pltpu.CompilerParams(collective_id=0, has_side_effects=True,
+                                             vmem_limit_bytes=8 * 1024 * 1024),
         name="gather",
     )(dynamics, observed.T, obs_index[None, :], obs_noise[None, :])
     bf, f32 = jnp.bfloat16, jnp.float32
@@ -330,7 +331,7 @@
             + [pltpu.VMEM((groups * width, LANES), bf)] * 4
             + [pltpu.VMEM((8 * groups, LANES), f32)] * 2
             + [pltpu.VMEM((8 * (chunks + 1), width), f32)] * 3),
-        compiler_params=pltpu.CompilerParams(vmem_limit_bytes=56 * 1024 * 1024),
+        compiler_params=pltpu.CompilerParams(vmem_limit_bytes=(20 + 12 * groups) * 1024 * 1024 if groups == 1 else 56 * 1024 * 1024),
         name="smooth",
     )(full, pattern, initial_mean, gathered)
     return filtered, smoothed

time: 33.2 us -> 32.5 us (0.979)
  Pallas kernels: 32.4 us -> 29.3 us
  local copies, waits for them, and re-layouts: 0 us -> 2.28 us
    pallas_call x1, Pallas kernels: 16.9 us -> 14.5 us  [per_device(): pl.pallas_call(functools.partial(gather_kernel, members, segments), out_s...]
    unnamed x0 -> x12, local copies, waits for them, and re-layouts: none -> 2.28 us
    pallas_call x1, Pallas kernels: 15.5 us -> 14.8 us  [per_device(): pl.pallas_call(functools.partial(compute_kernel, steps), out_shape=(out,...]
where the time goes in v6:
time: 32.5 us; the launch traced here: 32.3 us
  Pallas kernels  29.3 us (90%)
  local copies, waits for them, and re-layouts  2.28 us (7%)
  between operations  0.68 us (2%)
    pallas_call x1, Pallas kernels, per_device(): pl.pallas_call(functools.partial(compute_kernel, steps), out_shape=(out,...  14.8 us
    pallas_call x1, Pallas kernels, per_device(): pl.pallas_call(functools.partial(gather_kernel, members, segments), out_s...  14.5 us
    unnamed x12, local copies, waits for them, and re-layouts  2.28 us

profile of v6, /device:TPU:0, one launch (start us, length us, event | category | flops | bytes accessed | tf_op | source)
XLA Modules:
  0.0 32.3 jit_solution(13000199595633416806)
XLA Ops:
  0.6 0.0 copy-start.2
  0.6 0.0 copy-start.4
  0.7 0.0 copy-start.5
  0.7 0.7 %copy-done.2 = f32[16,4]{0,1:T(4,128)S(1)} copy-done((f32[16,4]{0,1:T(4,128)S(1)}, f32[16,4]{0,1:T(4,128)}, u32[]{:S(2)}) %copy-start.2) | copy-done | bytes 280
  1.3 0.0 copy-done.4
  1.3 0.0 copy-done.5
  1.3 0.0 copy-start
  1.3 0.9 %copy-done = f32[128,512]{1,0:T(8,128)S(1)} copy-done((f32[128,512]{1,0:T(8,128)S(1)}, f32[128,512]{1,0:T(8,128)}, u32[]{:S(2)}) %copy-start) | copy-done | bytes 262168
  2.3 0.0 copy-start.1
  2.3 14.5 %gather.1 = (f32[512,512]{1,0:T(8,128)S(1)}, f32[128,128]{1,0:T(8,128)S(1)}) custom-call(f32[128,512]{1,0:T(8,128)S(1)} %copy-done, f32[4,16]{1,0:T(4,128)S(1)} %bitcast.3, s32[1,16]{1,0:T(1,128)S(1)} %bitcast.4, f32[1,16]{1,0:T(1,128)S(1)} %bitcast.5), custom_call_target="tpu_custom_call" | custom-call | tf_op jit(solution)/shard_map/gather/pallas_call | solution.py:304
  16.8 0.0 copy-start.3
  16.8 0.0 copy-done.1
  16.8 0.7 %copy-done.3 = s32[4,4]{1,0:T(4,128)S(1)} copy-done((s32[4,4]{1,0:T(4,128)S(1)}, s32[4,4]{1,0:T(4,128)}, u32[]{:S(2)}) %copy-start.3) | copy-done | bytes 88
  17.4 14.8 %smooth.1 = (f32[16,1,512]{2,1,0:T(1,128)}, f32[16,1,512]{2,1,0:T(1,128)}) custom-call(f32[512,512]{1,0:T(8,128)S(1)} %get-tuple-element.4.full_ref, s32[4,4]{1,0:T(4,128)S(1)} %copy-done.3, f32[4,512]{1,0:T(4,128)S(1)} %copy-done.1, f32[128,128]{1,0:T(8,128)S(1)} %get-tuple-element.5.obs_ref), custom_call_target="tpu_custom_call" | custom-call | tf_op jit(solution)/shard_map/smooth/pallas_call | solution.py:320
Async XLA Ops:
  0.6 0.7 %copy-start.2 = (f32[16,4]{0,1:T(4,128)S(1)}, f32[16,4]{0,1:T(4,128)}, u32[]{:S(2)}) copy-start(f32[16,4]{0,1:T(4,128)} %param.9) | copy-start | bytes 772
  0.6 0.7 %copy-start.4 = (s32[16]{0:T(128)S(1)}, s32[16]{0:T(128)}, u32[]{:S(2)}) copy-start(s32[16]{0:T(128)} %param.10) | copy-start | bytes 196
  0.7 0.7 %copy-start.5 = (f32[16]{0:T(128)S(1)}, f32[16]{0:T(128)}, u32[]{:S(2)}) copy-start(f32[16]{0:T(128)} %param.11) | copy-start | bytes 196
  1.3 1.0 %copy-start = (f32[128,512]{1,0:T(8,128)S(1)}, f32[128,512]{1,0:T(8,128)}, u32[]{:S(2)}) copy-start(f32[128,512]{1,0:T(8,128)} %dyn_ref.1) | copy-start | bytes 786436
  2.3 14.5 %copy-start.1 = (f32[4,512]{1,0:T(4,128)S(1)}, f32[4,512]{1,0:T(4,128)}, u32[]{:S(2)}) copy-start(f32[4,512]{1,0:T(4,128)} %mean_ref.1) | copy-start | bytes 24580
  16.8 0.7 %copy-start.3 = (s32[4,4]{1,0:T(4,128)S(1)}, s32[4,4]{1,0:T(4,128)}, u32[]{:S(2)}) copy-start(s32[4,4]{1,0:T(4,128)} %pattern_ref.1) | copy-start | bytes 196
